TPU v7x, 32 devices: a whole 2x2x4 slice. The times are simulated.
32 devices in a mesh: fsdp: 4 (over z), expert: 8 (over y, x, core).
Axes of the slice: x: 2, y: 2, z: 4, core: 2. Of those that a mesh axis runs over, the one named last changes fastest.
Arguments:
- tokens: bfloat16 [512, 6144], P('expert', 'fsdp'), may hold values from -6 to 6
- expert_ids: int32 [512, 2], P('expert'), may hold values from 0 to 7, all different within a row; in each aligned block of 64 rows (0 to 63, 64 to 127, ...) at most 24 rows name the same one
- gate_values: float32 [512, 2], P('expert'), may hold values from 0.1 to 1
- w_gate: bfloat16 [6144, 65536], P('fsdp', 'expert'), may hold values from -0.078125 to 0.078125
- w_up: bfloat16 [6144, 65536], P('fsdp', 'expert'), may hold values from -0.078125 to 0.078125
- w_down: bfloat16 [65536, 6144], P('expert', 'fsdp'), may hold values from -0.0625 to 0.0625
- scale_gate: float32 [48, 512], P('fsdp', 'expert'), may hold values from 0.5 to 2
- scale_up: float32 [48, 512], P('fsdp', 'expert'), may hold values from 0.5 to 2
- scale_down: float32 [512, 48], P('expert', 'fsdp'), may hold values from 0.5 to 2
Outputs:
- mixed: bfloat16 [512, 6144], P('expert', 'fsdp')
Inputs may be any that keep to these rules, and one draw needn't show every extreme that they name: `expert_ids`: within the 64 rows of each index of expert (aligned blocks of rows), no expert id occurs in more than 24 rows, and some id occurs in exactly 24 rows of some block; the two ids of a row differ; every id occurs somewhere.
All inputs are finite; a program needn't handle non-finite values.
Results may differ from a plain program's by a relative error of at most 0.03.
Values may be sent and summed in bfloat16 or wider, within the bound.
No kernel may reach another device: no remote copies, remote signals or barrier semaphores. Data moves between devices by JAX's collectives and lax.ppermute only.
A program may use at most 192 MiB of HBM per device.

v0:
```python
import jax
import jax.numpy as jnp
from jax import lax
from jax.sharding import PartitionSpec as P

EXPERTS = 8
BLOCK = 128
CAP = 24


def rounded(values):
    return lax.optimization_barrier(values.astype(jnp.bfloat16)).astype(jnp.float32)


def dequant(weights, block_scale):
    spread = jnp.repeat(jnp.repeat(block_scale, BLOCK, axis=0), BLOCK, axis=1)
    return (weights.astype(jnp.float32) * spread).astype(jnp.bfloat16)


def shards(tokens, expert_ids, gate_values, w_gate, w_up, w_down, scale_gate, scale_up, scale_down):
    device_count = lax.axis_size("expert")
    slices = device_count // EXPERTS
    local_tokens = tokens.shape[0]
    feature_cols = tokens.shape[1]
    slot_total = EXPERTS * CAP
    flat_ids = expert_ids.reshape(-1)
    onehot = (flat_ids[:, None] == jnp.arange(EXPERTS, dtype=jnp.int32)[None, :]).astype(jnp.int32)
    slot_rank = jnp.sum((jnp.cumsum(onehot, axis=0) - onehot) * onehot, axis=1)
    target = flat_ids * CAP + slot_rank
    placing = (target[:, None] == jnp.arange(slot_total, dtype=jnp.int32)[None, :]).astype(
        jnp.float32
    )
    token_map = jnp.sum(placing.reshape(local_tokens, 2, slot_total), axis=1).astype(jnp.bfloat16)
    packed = jnp.einsum("ts,td->sd", token_map, tokens, preferred_element_type=jnp.float32).astype(
        jnp.bfloat16
    )
    outgoing = jnp.broadcast_to(
        packed.reshape(EXPERTS, 1, CAP, feature_cols), (EXPERTS, slices, CAP, feature_cols)
    ).reshape(device_count * CAP, feature_cols)
    incoming = lax.all_to_all(outgoing, "expert", split_axis=0, concat_axis=0, tiled=True)
    down_deq = dequant(w_down, scale_down)

    def make_term(weights):
        return rounded(jnp.dot(incoming, weights, preferred_element_type=jnp.float32))

    gate_sum = lax.psum_scatter(
        make_term(dequant(w_gate, scale_gate)).astype(jnp.bfloat16),
        "fsdp",
        scatter_dimension=0,
        tiled=True,
    ).astype(jnp.float32)
    up_sum = lax.psum_scatter(
        make_term(dequant(w_up, scale_up)).astype(jnp.bfloat16),
        "fsdp",
        scatter_dimension=0,
        tiled=True,
    ).astype(jnp.float32)
    hidden = (jax.nn.silu(gate_sum) * up_sum).astype(jnp.bfloat16)
    partial_rows = jnp.dot(
        lax.all_gather(hidden, "fsdp", axis=0, tiled=True),
        down_deq,
        preferred_element_type=jnp.float32,
    ).astype(jnp.bfloat16)
    returned = lax.all_to_all(partial_rows, "expert", split_axis=0, concat_axis=0, tiled=True)
    slice_sums = jnp.sum(
        returned.reshape(EXPERTS, slices, CAP, feature_cols).astype(jnp.float32), axis=1
    )
    slice_sums = slice_sums.reshape(slot_total, feature_cols)
    weights_map = jnp.sum(
        (placing * gate_values.reshape(-1)[:, None]).reshape(local_tokens, 2, slot_total), axis=1
    )
    mixed_rows = jnp.dot(
        weights_map, slice_sums, precision=lax.Precision.HIGHEST, preferred_element_type=jnp.float32
    )
    return mixed_rows.astype(jnp.bfloat16)


def solution(mesh):
    in_specs = (
        P("expert", "fsdp"),
        P("expert", None),
        P("expert", None),
        P("fsdp", "expert"),
        P("fsdp", "expert"),
        P("expert", "fsdp"),
        P("fsdp", "expert"),
        P("fsdp", "expert"),
        P("expert", "fsdp"),
    )
    out_specs = P("expert", "fsdp")
    return jax.shard_map(shards, mesh=mesh, in_specs=in_specs, out_specs=out_specs, check_vma=False)
```

profile of v0, /device:TPU:0, one launch (start us, length us, event | category | flops | bytes accessed | tf_op | source)
XLA Modules:
  0.0 324.4 jit_solution(10470059217898736720)
XLA Ops:
  6.5 0.8 copy.25
  7.6 0.2 reduce_window_sum.11
  7.8 0.2 select_reduce_fusion.1
  8.2 0.7 multiply_add_fusion
  8.8 0.8 convert_reduce_fusion
  9.7 0.3 convolution_convert_fusion
  10.0 15.4 %all_to_all.24 = bf16[8,24,1536]{2,1,0:T(8,128)(2,1)S(1)} all-to-all(bf16[8,24,1536]{2,1,0:T(8,128)(2,1)S(1)} %bitcast.47), channel_id=1, replica_groups=mesh['fsdp'=4,'expert'=8] {'expert'}, dimensions={0} | all-to-all | bytes 1179648 | tf_op jit(solution)/shard_map/all_to_all | solution.py:40
  25.4 0.7 broadcast_in_dim.23
  26.2 16.5 %broadcast_in_dim.24 = f32[1536,64,128]{2,1,0:T(8,128)} broadcast(f32[1536,64]{1,0:T(8,128)S(1)} %bitcast.44), dimensions={0,1} | broadcast | bytes 50724864 | tf_op jit(solution)/shard_map/broadcast_in_dim | solution.py:16
  42.6 51.4 %fusion.7 = bf16[192,8192]{1,0:T(8,128)(2,1)} fusion(bf16[192,1536]{1,0:T(8,128)(2,1)S(1)} %bitcast.42, f32[192,8,64,128]{3,2,1,0:T(8,128)} %bitcast.41, bf16[1536,8192]{1,0:T(8,128)(2,1)} %param.13), kind=kOutput, calls=%fused_computation.8 | convolution fusion | flops 4871159808 | bytes 79233024 | tf_op jit(solution)/shard_map/dot_general | solution.py:44
  94.1 0.2 reduce-scatter.3.cloned.1.call-start
  94.4 16.6 %broadcast_in_dim.22 = f32[1536,64,128]{2,1,0:T(8,128)} broadcast(f32[1536,64]{1,0:T(8,128)S(1)} %bitcast.45), dimensions={0,1} | broadcast | bytes 50724864 | tf_op jit(solution)/shard_map/broadcast_in_dim | solution.py:16
  110.9 51.5 %fusion.10 = bf16[192,8192]{1,0:T(8,128)(2,1)} fusion(bf16[192,1536]{1,0:T(8,128)(2,1)S(1)} %bitcast.43, f32[192,8,64,128]{3,2,1,0:T(8,128)} %bitcast.40, bf16[1536,8192]{1,0:T(8,128)(2,1)} %param.12), kind=kOutput, calls=%fused_computation.9 | convolution fusion | flops 4871159808 | bytes 79233024 | tf_op jit(solution)/shard_map/dot_general | solution.py:44
  162.5 0.3 all-gather.2.cloned.1.call-start
  162.8 59.5 %reduce-scatter.3.cloned.1.call-done = bf16[48,8192]{1,0:T(8,128)(2,1)} async-done(((bf16[192,8192]{1,0:T(8,128)(2,1)}), bf16[48,8192]{1,0:T(8,128)(2,1)}) %reduce-scatter.3.cloned.1.call-update) | async-done | bytes 786448 | tf_op jit(solution)/shard_map/reduce_scatter | solution.py:46
  222.3 2.7 fusion.17
  225.0 32.8 %copy.27 = bf16[8192,1536]{0,1:T(8,128)(2,1)} copy(bf16[8192,1536]{1,0:T(8,128)(2,1)} %param.14) | data formatting | bytes 50331648 | tf_op args[5]
  257.8 0.2 broadcast_bitcast_fusion
  258.0 0.3 copy.30
  258.3 22.7 %fusion.2 = bf16[8192,1536]{0,1:T(8,128)(2,1)} fusion(bf16[8192,1536]{0,1:T(8,128)(2,1)} %copy.27, f32[8192,12]{0,1:T(8,128)S(1)} %bitcast.48), kind=kLoop, calls=%fused_computation.5 | loop fusion | flops 37748736 | bytes 50724864 | tf_op jit(solution)/shard_map/convert_element_type | solution.py:17
  281.1 7.6 %all-gather.2.cloned.1.call-done = bf16[192,8192]{1,0:T(8,128)(2,1)} async-done(((bf16[48,8192]{1,0:T(8,128)(2,1)}), bf16[192,8192]{1,0:T(8,128)(2,1)}) %all-gather.2.cloned.1.call-update) | async-done | bytes 3145744 | tf_op jit(solution)/shard_map/all_gather | solution.py:60
  288.7 14.2 %convolution_convert_fusion.1 = bf16[192,1536]{1,0:T(8,128)(2,1)S(1)} fusion(bf16[192,8192]{1,0:T(8,128)(2,1)} %all-gather.2.cloned.1.call-done, bf16[8192,1536]{0,1:T(8,128)(2,1)} %fusion.2), kind=kOutput, calls=%fused_computation.11 | convolution fusion | flops 4832133120 | bytes 28901376 | tf_op jit(solution)/shard_map/dot_general | solution.py:59
  302.9 13.9 %all_to_all.25 = bf16[8,24,1536]{2,1,0:T(8,128)(2,1)S(1)} all-to-all(bf16[8,24,1536]{2,1,0:T(8,128)(2,1)S(1)} %bitcast.50), channel_id=1, replica_groups=mesh['fsdp'=4,'expert'=8] {'expert'}, dimensions={0} | all-to-all | bytes 1179648 | tf_op jit(solution)/shard_map/all_to_all | solution.py:64
  316.8 1.1 convolution_convert_fusion.2
  (19 shorter events, 0.6 us)
Async XLA Ops:
  6.5 3.1 copy-start
  6.5 156.2 %reduce-scatter.5.cloned.1.call-start = ((), (), s32[]{:S(2)}) async-start(), calls=%async_computation.5 | async-start | bytes 3932160 | tf_op jit(solution)/shard_map/reduce_scatter | solution.py:52
  42.6 51.7 %copy-start.2 = (f32[12,64]{1,0:T(8,128)S(1)}, f32[12,64]{1,0:T(8,128)}, u32[]{:S(2)}) copy-start(f32[12,64]{1,0:T(8,128)} %param.15) | copy-start | bytes 9220
  94.1 128.2 %reduce-scatter.3.cloned.1.call-start = ((), (), s32[]{:S(2)}) async-start(), calls=%async_computation.4 | async-start | bytes 3932160 | tf_op jit(solution)/shard_map/reduce_scatter | solution.py:46
  162.5 126.2 %all-gather.2.cloned.1.call-start = ((), (), s32[]{:S(2)}) async-start(), calls=%async_computation.6 | async-start | bytes 3932160 | tf_op jit(solution)/shard_map/all_gather | solution.py:60
  225.0 32.8 %copy-start.3 = (f32[64,12]{0,1:T(8,128)S(1)}, f32[64,12]{0,1:T(8,128)}, u32[]{:S(2)}) copy-start(f32[64,12]{0,1:T(8,128)} %param.17) | copy-start | bytes 9220
  258.3 59.6 %copy-start.1 = (bf16[64,1536]{1,0:T(8,128)(2,1)S(1)}, bf16[64,1536]{1,0:T(8,128)(2,1)}, u32[]{:S(2)}) copy-start(bf16[64,1536]{1,0:T(8,128)(2,1)} %param.9) | copy-start | bytes 589828
Sparse Core Ops, SparseCore 0:
  94.2 59.6 reduce-scatter.4
  162.6 59.6 reduce-scatter.2
  225.1 63.5 all-gather.1
where the time goes:
time: 326 us; the launch traced here: 324 us
  matrix products  119 us (37%)
  local copies, waits for them, and re-layouts  68.3 us (21%)
  waiting for transfers between devices  67.2 us (21%)
  blocking collectives  29.3 us (9%)
  other arithmetic  27.3 us (8%)
  between operations  13.2 us (4%)
    dot_general x2, matrix products, make_term(): jnp.dot(incoming, weights, preferred_element_type=jnp.float32)  103 us
    reduce_scatter x1, waiting for transfers between devices, shards(): lax.psum_scatter(make_term(dequant(w_gate, scale_gate)).astype(jnp.bfloat...  59.5 us
    unnamed x13, local copies, waits for them, and re-layouts  34.1 us
    broadcast_in_dim x4, local copies, waits for them, and re-layouts, dequant(): spread = jnp.repeat(jnp.repeat(block_scale, BLOCK, axis=0), BLOCK, axis=1)  33.8 us
    convert_element_type x1, other arithmetic, dequant(): return (weights.astype(jnp.float32) * spread).astype(jnp.bfloat16)  22.7 us
    all_to_all x1, blocking collectives, shards(): lax.all_to_all(outgoing, 'expert', split_axis=0, concat_axis=0, tiled=True)  15.4 us
    dot_general x1, matrix products, shards(): jnp.dot(lax.all_gather(hidden, 'fsdp', axis=0, tiled=True), down_deq, pre...  14.2 us
    all_to_all x1, blocking collectives, shards(): lax.all_to_all(partial_rows, 'expert', split_axis=0, concat_axis=0, tiled...  13.9 us
  transfers between devices with their start and end apart: 3, of which 2 were waited for; matrix products, arithmetic and copies ran while one was open for 38% of the time, Pallas kernels for 0%

commit v1 on v0

--- a/solution.py
+++ b/solution.py
@@ -1,20 +1,134 @@
+import functools
+
 import jax
 import jax.numpy as jnp
 from jax import lax
+from jax.experimental import pallas as pl
+from jax.experimental.pallas import tpu as pltpu
 from jax.sharding import PartitionSpec as P
 
 EXPERTS = 8
 BLOCK = 128
 CAP = 24
+CHUNKS = 4
 
 
-def rounded(values):
-    return lax.optimization_barrier(values.astype(jnp.bfloat16)).astype(jnp.float32)
+def widen(block_scale):
+    return jnp.repeat(block_scale, BLOCK, axis=1).astype(jnp.bfloat16)
 
 
-def dequant(weights, block_scale):
-    spread = jnp.repeat(jnp.repeat(block_scale, BLOCK, axis=0), BLOCK, axis=1)
-    return (weights.astype(jnp.float32) * spread).astype(jnp.bfloat16)
+def spread(weights, scale_rows):
+    depth, width = weights.shape
+    parts = [
+        weights[k * BLOCK : (k + 1) * BLOCK, :] * scale_rows[k : k + 1, :]
+        for k in range(depth // BLOCK)
+    ]
+    return jnp.concatenate(parts, axis=0) if len(parts) > 1 else parts[0]
+
+
+def own_kernel(index_ref, x_ref, gate_ref, up_ref, gate_scale_ref, up_scale_ref, out_ref):
+    x = x_ref[...]
+    out_ref[0] = jnp.dot(
+        x, spread(gate_ref[...], gate_scale_ref[...]), preferred_element_type=jnp.float32
+    ).astype(jnp.bfloat16)
+    out_ref[1] = jnp.dot(
+        x, spread(up_ref[...], up_scale_ref[...]), preferred_element_type=jnp.float32
+    ).astype(jnp.bfloat16)
+
+
+def own_terms(index, x, w_gate, w_up, gate_scale, up_scale, chunk):
+    rows, depth = x.shape
+    width = min(256, chunk)
+    steps = chunk // width
+    column = lambda j, index: (0, index[0] * steps + j)
+    weight_spec = pl.BlockSpec((depth, width), column)
+    scale_spec = pl.BlockSpec((depth // BLOCK, width), column)
+    return pl.pallas_call(
+        own_kernel,
+        grid_spec=pltpu.PrefetchScalarGridSpec(
+            num_scalar_prefetch=1,
+            grid=(steps,),
+            in_specs=[
+                pl.BlockSpec((rows, depth), lambda j, index: (0, 0)),
+                weight_spec,
+                weight_spec,
+                scale_spec,
+                scale_spec,
+            ],
+            out_specs=pl.BlockSpec((2, rows, width), lambda j, index: (0, 0, j)),
+        ),
+        out_shape=jax.ShapeDtypeStruct((2, rows, chunk), jnp.bfloat16),
+        compiler_params=pltpu.CompilerParams(vmem_limit_bytes=32 * 1024 * 1024),
+        cost_estimate=pl.CostEstimate(
+            flops=4 * rows * depth * chunk, bytes_accessed=4 * depth * chunk, transcendentals=0
+        ),
+        name="gate_up",
+    )(index, x, w_gate, w_up, gate_scale, up_scale)
+
+
+def down_kernel(index_ref, hidden_ref, weight_ref, scale_ref, total_ref, out_ref):
+    step = pl.program_id(0)
+
+    @pl.when(step == 0)
+    def _():
+        out_ref[...] = total_ref[...]
+
+    @pl.when(index_ref[1] > 0)
+    def _():
+        out_ref[...] += jnp.dot(
+            hidden_ref[...],
+            spread(weight_ref[...], scale_ref[0]),
+            preferred_element_type=jnp.float32,
+        )
+
+
+def down_add(index, hidden, w_down, down_scale, total):
+    rows, chunk = hidden.shape
+    width = w_down.shape[1]
+    depth = min(256, chunk)
+    steps = chunk // depth
+    at = lambda j, index: index[0] * steps + jnp.where(index[1] > 0, j, 0)
+    scale = down_scale.reshape(-1, depth // BLOCK, width)
+    return pl.pallas_call(
+        down_kernel,
+        grid_spec=pltpu.PrefetchScalarGridSpec(
+            num_scalar_prefetch=1,
+            grid=(steps,),
+            in_specs=[
+                pl.BlockSpec((rows, depth), lambda j, index: (0, j)),
+                pl.BlockSpec((depth, width), lambda j, index: (at(j, index), 0)),
+                pl.BlockSpec((1, depth // BLOCK, width), lambda j, index: (at(j, index), 0, 0)),
+                pl.BlockSpec((rows, width), lambda j, index: (0, 0)),
+            ],
+            out_specs=pl.BlockSpec((rows, width), lambda j, index: (0, 0)),
+        ),
+        out_shape=jax.ShapeDtypeStruct((rows, width), jnp.float32),
+        input_output_aliases={4: 0},
+        compiler_params=pltpu.CompilerParams(vmem_limit_bytes=32 * 1024 * 1024),
+        cost_estimate=pl.CostEstimate(
+            flops=2 * rows * width * chunk, bytes_accessed=2 * width * chunk, transcendentals=0
+        ),
+        name="down",
+    )(index, hidden, w_down, scale, total)
+
+
+def activate(gate, up):
+    gate, up = gate.astype(jnp.float32), up.astype(jnp.float32)
+    return (jax.nn.silu(gate) * up).astype(jnp.bfloat16)
+
+
+def expert_rows(x, w_gate, w_up, w_down, gate_scale, up_scale, down_scale):
+    hidden_width = w_gate.shape[1]
+    chunk = hidden_width // CHUNKS
+    total = jnp.zeros((x.shape[0], w_down.shape[1]), jnp.float32)
+    sums = []
+    for c in range(CHUNKS):
+        own = own_terms(jnp.array([c], jnp.int32), x, w_gate, w_up, gate_scale, up_scale, chunk)
+        sums.append(lax.psum_scatter(own, "fsdp", scatter_dimension=1, tiled=True))
+    for c in range(CHUNKS):
+        hidden = lax.all_gather(activate(sums[c][0], sums[c][1]), "fsdp", axis=0, tiled=True)
+        total = down_add(jnp.array([c, 1], jnp.int32), hidden, w_down, down_scale, total)
+    return total
 
 
 def shards(tokens, expert_ids, gate_values, w_gate, w_up, w_down, scale_gate, scale_up, scale_down):
@@ -38,28 +152,8 @@
         packed.reshape(EXPERTS, 1, CAP, feature_cols), (EXPERTS, slices, CAP, feature_cols)
     ).reshape(device_count * CAP, feature_cols)
     incoming = lax.all_to_all(outgoing, "expert", split_axis=0, concat_axis=0, tiled=True)
-    down_deq = dequant(w_down, scale_down)
-
-    def make_term(weights):
-        return rounded(jnp.dot(incoming, weights, preferred_element_type=jnp.float32))
-
-    gate_sum = lax.psum_scatter(
-        make_term(dequant(w_gate, scale_gate)).astype(jnp.bfloat16),
-        "fsdp",
-        scatter_dimension=0,
-        tiled=True,
-    ).astype(jnp.float32)
-    up_sum = lax.psum_scatter(
-        make_term(dequant(w_up, scale_up)).astype(jnp.bfloat16),
-        "fsdp",
-        scatter_dimension=0,
-        tiled=True,
-    ).astype(jnp.float32)
-    hidden = (jax.nn.silu(gate_sum) * up_sum).astype(jnp.bfloat16)
-    partial_rows = jnp.dot(
-        lax.all_gather(hidden, "fsdp", axis=0, tiled=True),
-        down_deq,
-        preferred_element_type=jnp.float32,
+    partial_rows = expert_rows(
+        incoming, w_gate, w_up, w_down, widen(scale_gate), widen(scale_up), widen(scale_down)
     ).astype(jnp.bfloat16)
     returned = lax.all_to_all(partial_rows, "expert", split_axis=0, concat_axis=0, tiled=True)
     slice_sums = jnp.sum(

time: 326 us -> 278 us (0.85)
  matrix products: 119 us -> 2.25 us
  blocking collectives: 29.3 us -> 111 us
  Pallas kernels: 0 us -> 67.2 us
  local copies, waits for them, and re-layouts: 68.3 us -> 3.1 us
  other arithmetic: 27.3 us -> 6.55 us
  starting transfers between devices: 0.49 us -> 5.33 us
    dot_general x3 -> x0, matrix products: 117 us -> none  [the longest x2 103 us: make_term(): jnp.dot(incoming, weights, preferred_element_type=jnp.float32)]
    all_gather x0 -> x4, blocking collectives: none -> 96.9 us  [expert_rows(): lax.all_gather(activate(sums[c][0], sums[c][1]), 'fsdp', axis=0, tiled=True)]
    pallas_call x0 -> x8, Pallas kernels: none -> 67.2 us  [the longest x4 38 us: own_terms(): pl.pallas_call(own_kernel, grid_spec=pltpu.PrefetchScalarGridSpec(num_sca...]
    broadcast_in_dim x4, local copies, waits for them, and re-layouts: 33.8 us -> 0.64 us  [the longest x3 0.53 us: widen(): return jnp.repeat(block_scale, BLOCK, axis=1).astype(jnp.bfloat16)]
    unnamed x13 -> x19, local copies, waits for them, and re-layouts: 34.1 us -> 1.91 us
    convert_element_type x2 -> x8, other arithmetic: 25.4 us -> 4.63 us  [the longest x4 4.56 us: activate(): return (jax.nn.silu(gate) * up).astype(jnp.bfloat16)]
    all_to_all x1 -> x0, blocking collectives: 15.4 us -> none  [shards(): lax.all_to_all(outgoing, 'expert', split_axis=0, concat_axis=0, tiled=True)]
    all_to_all x0 -> x1, waiting for transfers between devices: none -> 9.59 us  [shards(): lax.all_to_all(outgoing, 'expert', split_axis=0, concat_axis=0, tiled=True)]
  transfers between devices with their start and end apart: 3 -> 5, of which waited for: 2 -> 5; matrix products, arithmetic and copies ran while one was open for 38% -> 2% of each run, Pallas kernels for 0% -> 10%
where the time goes in v1:
time: 278 us; the launch traced here: 277 us
  blocking collectives  111 us (40%)
  waiting for transfers between devices  68 us (24%)
  Pallas kernels  67.2 us (24%)
  between operations  13.4 us (5%)
  other arithmetic  6.55 us (2%)
  starting transfers between devices  5.33 us (2%)
  local copies, waits for them, and re-layouts  3.1 us (1%)
    all_gather x4, blocking collectives, expert_rows(): lax.all_gather(activate(sums[c][0], sums[c][1]), 'fsdp', axis=0, tiled=True)  96.9 us
    reduce_scatter x4, waiting for transfers between devices, expert_rows(): sums.append(lax.psum_scatter(own, 'fsdp', scatter_dimension=1, tiled=True))  58.4 us
    pallas_call x4, Pallas kernels, own_terms(): pl.pallas_call(own_kernel, grid_spec=pltpu.PrefetchScalarGridSpec(num_sca...  38 us
    pallas_call x4, Pallas kernels, down_add(): pl.pallas_call(down_kernel, grid_spec=pltpu.PrefetchScalarGridSpec(num_sc...  29.2 us
    all_to_all x1, blocking collectives, shards(): lax.all_to_all(partial_rows, 'expert', split_axis=0, concat_axis=0, tiled...  14 us
    all_to_all x1, waiting for transfers between devices, shards(): lax.all_to_all(outgoing, 'expert', split_axis=0, concat_axis=0, tiled=True)  9.59 us
  transfers between devices with their start and end apart: 5, of which 5 were waited for; matrix products, arithmetic and copies ran while one was open for 2% of the time, Pallas kernels for 10%

profile of v1, /device:TPU:0, one launch (start us, length us, event | category | flops | bytes accessed | tf_op | source)
XLA Modules:
  0.0 276.8 jit_solution(15229560450505127916)
XLA Ops:
  9.7 1.1 convolution_convert_fusion
  10.8 5.2 %all-to-all-start = ((bf16[8,24,1536]{2,1,0:T(8,128)(2,1)}), bf16[8,24,1536]{2,1,0:T(8,128)(2,1)S(1)}, u32[]{:S(2)}, u32[]{:S(2)}) async-start(bf16[8,24,1536]{2,1,0:T(8,128)(2,1)} %bitcast), calls=%async_computation | async-start | bytes 1179648 | tf_op jit(solution)/shard_map/all_to_all | solution.py:154
  16.8 9.6 %all-to-all-done = bf16[8,24,1536]{2,1,0:T(8,128)(2,1)S(1)} async-done(((bf16[8,24,1536]{2,1,0:T(8,128)(2,1)}), bf16[8,24,1536]{2,1,0:T(8,128)(2,1)S(1)}, u32[]{:S(2)}, u32[]{:S(2)}) %all-to-all-start) | async-done | bytes 589856 | tf_op jit(solution)/shard_map/all_to_all | solution.py:154
  26.4 9.4 %gate_up.7 = bf16[2,192,2048]{2,1,0:T(8,128)(2,1)} custom-call(s32[1]{0:T(128)} %constant.34.clone.index_ref, bf16[192,1536]{1,0:T(8,128)(2,1)S(1)} %bitcast.54, bf16[1536,8192]{1,0:T(8,128)(2,1)} %gate_ref.7, bf16[1536,8192]{1,0:T(8,128)(2,1)} %up_ref.7, bf16[12,8192]{1,0:T(8,128)(2,1)S(1)} %bitcast.58, bf16[12,8192]{1,0:T(8,128)(2,1)S(1)} %bitcast.62), custom_call_target="tpu_custom_call" | custom-call | flops 2415919104 | bytes 12582912 | tf_op jit(solution)/shard_map/gate_up/pallas_call | solution.py:46
  35.9 9.6 %gate_up.6 = bf16[2,192,2048]{2,1,0:T(8,128)(2,1)} custom-call(s32[1]{0:T(128)} %constant.35.clone.index_ref, bf16[192,1536]{1,0:T(8,128)(2,1)S(1)} %bitcast.55, bf16[1536,8192]{1,0:T(8,128)(2,1)} %gate_ref.7, bf16[1536,8192]{1,0:T(8,128)(2,1)} %up_ref.7, bf16[12,8192]{1,0:T(8,128)(2,1)S(1)} %bitcast.59, bf16[12,8192]{1,0:T(8,128)(2,1)S(1)} %bitcast.63), custom_call_target="tpu_custom_call" | custom-call | flops 2415919104 | bytes 12582912 | tf_op jit(solution)/shard_map/gate_up/pallas_call | solution.py:46
  45.6 9.4 %gate_up.5 = bf16[2,192,2048]{2,1,0:T(8,128)(2,1)} custom-call(s32[1]{0:T(128)} %constant.36.clone.index_ref, bf16[192,1536]{1,0:T(8,128)(2,1)S(1)} %bitcast.56, bf16[1536,8192]{1,0:T(8,128)(2,1)} %gate_ref.7, bf16[1536,8192]{1,0:T(8,128)(2,1)} %up_ref.7, bf16[12,8192]{1,0:T(8,128)(2,1)S(1)} %bitcast.60, bf16[12,8192]{1,0:T(8,128)(2,1)S(1)} %bitcast.64), custom_call_target="tpu_custom_call" | custom-call | flops 2415919104 | bytes 12582912 | tf_op jit(solution)/shard_map/gate_up/pallas_call | solution.py:46
  55.1 9.5 %gate_up.4 = bf16[2,192,2048]{2,1,0:T(8,128)(2,1)} custom-call(s32[1]{0:T(128)} %constant.37.clone.index_ref, bf16[192,1536]{1,0:T(8,128)(2,1)S(1)} %bitcast.57, bf16[1536,8192]{1,0:T(8,128)(2,1)} %gate_ref.7, bf16[1536,8192]{1,0:T(8,128)(2,1)} %up_ref.7, bf16[12,8192]{1,0:T(8,128)(2,1)S(1)} %bitcast.61, bf16[12,8192]{1,0:T(8,128)(2,1)S(1)} %bitcast.65), custom_call_target="tpu_custom_call" | custom-call | flops 2415919104 | bytes 12582912 | tf_op jit(solution)/shard_map/gate_up/pallas_call | solution.py:46
  65.8 4.9 %reduce-scatter.11.cloned.1.call-done = bf16[2,48,2048]{2,1,0:T(8,128)(2,1)} async-done(((bf16[2,192,2048]{2,1,0:T(8,128)(2,1)}), bf16[2,48,2048]{2,1,0:T(8,128)(2,1)}) %reduce-scatter.11.cloned.1.call-update) | async-done | bytes 393232 | tf_op jit(solution)/shard_map/reduce_scatter | solution.py:127
  70.7 1.1 fusion.16
  71.8 25.1 %all_gather.15.hidden_ref = bf16[192,2048]{1,0:T(8,128)(2,1)S(1)} all-gather(bf16[48,2048]{1,0:T(8,128)(2,1)S(1)} %fusion.16), channel_id=1, replica_groups=mesh['fsdp'=4,'expert'=8] {'fsdp'}, dimensions={0}, use_global_device_ids=true | all-gather | bytes 983040 | tf_op jit(solution)/shard_map/all_gather | solution.py:129
  97.0 17.7 %reduce-scatter.9.cloned.1.call-done = bf16[2,48,2048]{2,1,0:T(8,128)(2,1)} async-done(((bf16[2,192,2048]{2,1,0:T(8,128)(2,1)}), bf16[2,48,2048]{2,1,0:T(8,128)(2,1)}) %reduce-scatter.9.cloned.1.call-update) | async-done | bytes 393232 | tf_op jit(solution)/shard_map/reduce_scatter | solution.py:127
  114.7 1.1 fusion.17
  115.9 25.7 %all_gather.14.hidden_ref = bf16[192,2048]{1,0:T(8,128)(2,1)S(1)} all-gather(bf16[48,2048]{1,0:T(8,128)(2,1)S(1)} %fusion.17), channel_id=1, replica_groups=mesh['fsdp'=4,'expert'=8] {'fsdp'}, dimensions={0}, use_global_device_ids=true | all-gather | bytes 983040 | tf_op jit(solution)/shard_map/all_gather | solution.py:129
  141.6 17.9 %reduce-scatter.7.cloned.1.call-done = bf16[2,48,2048]{2,1,0:T(8,128)(2,1)} async-done(((bf16[2,192,2048]{2,1,0:T(8,128)(2,1)}), bf16[2,48,2048]{2,1,0:T(8,128)(2,1)}) %reduce-scatter.7.cloned.1.call-update) | async-done | bytes 393232 | tf_op jit(solution)/shard_map/reduce_scatter | solution.py:127
  159.5 1.1 fusion.18
  160.6 26.6 %all_gather.13.hidden_ref = bf16[192,2048]{1,0:T(8,128)(2,1)S(1)} all-gather(bf16[48,2048]{1,0:T(8,128)(2,1)S(1)} %fusion.18), channel_id=1, replica_groups=mesh['fsdp'=4,'expert'=8] {'fsdp'}, dimensions={0}, use_global_device_ids=true | all-gather | bytes 983040 | tf_op jit(solution)/shard_map/all_gather | solution.py:129
  187.2 17.8 %reduce-scatter.5.cloned.1.call-done = bf16[2,48,2048]{2,1,0:T(8,128)(2,1)} async-done(((bf16[2,192,2048]{2,1,0:T(8,128)(2,1)}), bf16[2,48,2048]{2,1,0:T(8,128)(2,1)}) %reduce-scatter.5.cloned.1.call-update) | async-done | bytes 393232 | tf_op jit(solution)/shard_map/reduce_scatter | solution.py:127
  205.0 1.1 fusion.19
  206.1 19.5 %all_gather.12.hidden_ref = bf16[192,2048]{1,0:T(8,128)(2,1)S(1)} all-gather(bf16[48,2048]{1,0:T(8,128)(2,1)S(1)} %fusion.19), channel_id=1, replica_groups=mesh['fsdp'=4,'expert'=8] {'fsdp'}, dimensions={0}, use_global_device_ids=true | all-gather | bytes 983040 | tf_op jit(solution)/shard_map/all_gather | solution.py:129
  225.8 7.3 %down.4.total_ref = f32[192,1536]{1,0:T(8,128)S(1)} custom-call(s32[2]{0:T(128)S(1)} %call_exported.0.index_ref, bf16[192,2048]{1,0:T(8,128)(2,1)S(1)} %all_gather.15.hidden_ref, bf16[8192,1536]{1,0:T(8,128)(2,1)} %weight_ref.7, bf16[32,2,1536]{2,1,0:T(2,128)(2,1)S(1)} %convert_element_type.112.scale_ref, ...), custom_call_target="tpu_custom_call", output_to_operand_aliasing={{}: (4, {})} | custom-call | flops 1207959552 | bytes 6291456 | tf_op jit(solution)/shard_map/down/pallas_call | solution.py:92
  233.1 7.3 %down.5.total_ref = f32[192,1536]{1,0:T(8,128)S(1)} custom-call(s32[2]{0:T(128)S(1)} %call_exported.1.index_ref, bf16[192,2048]{1,0:T(8,128)(2,1)S(1)} %all_gather.14.hidden_ref, bf16[8192,1536]{1,0:T(8,128)(2,1)} %weight_ref.7, bf16[32,2,1536]{2,1,0:T(2,128)(2,1)S(1)} %convert_element_type.112.scale_ref, ...), custom_call_target="tpu_custom_call", output_to_operand_aliasing={{}: (4, {})} | custom-call | flops 1207959552 | bytes 6291456 | tf_op jit(solution)/shard_map/down/pallas_call | solution.py:92
  240.4 7.3 %down.6.total_ref = f32[192,1536]{1,0:T(8,128)S(1)} custom-call(s32[2]{0:T(128)S(1)} %copy-done.3, bf16[192,2048]{1,0:T(8,128)(2,1)S(1)} %all_gather.13.hidden_ref, bf16[8192,1536]{1,0:T(8,128)(2,1)} %weight_ref.7, bf16[32,2,1536]{2,1,0:T(2,128)(2,1)S(1)} %convert_element_type.112.scale_ref, ...), custom_call_target="tpu_custom_call", output_to_operand_aliasing={{}: (4, {})} | custom-call | flops 1207959552 | bytes 6291456 | tf_op jit(solution)/shard_map/down/pallas_call | solution.py:92
  247.8 7.3 %down.7 = f32[192,1536]{1,0:T(8,128)S(1)} custom-call(s32[2]{0:T(128)S(1)} %copy-done.2, bf16[192,2048]{1,0:T(8,128)(2,1)S(1)} %all_gather.12.hidden_ref, bf16[8192,1536]{1,0:T(8,128)(2,1)} %weight_ref.7, bf16[32,2,1536]{2,1,0:T(2,128)(2,1)S(1)} %convert_element_type.112.scale_ref, f32[192,1536]{1,0:T(8,128)S(1)} %down.6.total_ref), custom_call_target="tpu_custom_call", output_to_operand_aliasing={{}: (4, {})} | custom-call | flops 1207959552 | bytes 6291456 | tf_op jit(solution)/shard_map/down/pallas_call | solution.py:92
  255.1 14.0 %all_to_all.23 = bf16[8,24,1536]{2,1,0:T(8,128)(2,1)S(1)} all-to-all(bf16[8,24,1536]{2,1,0:T(8,128)(2,1)S(1)} %bitcast.66), channel_id=1, replica_groups=mesh['fsdp'=4,'expert'=8] {'expert'}, dimensions={0} | all-to-all | bytes 1179648 | tf_op jit(solution)/shard_map/all_to_all | solution.py:158
  (48 shorter events, 6.4 us)
Async XLA Ops:
  6.5 3.1 %copy-start = (bf16[64,1536]{1,0:T(8,128)(2,1)S(1)}, bf16[64,1536]{1,0:T(8,128)(2,1)}, u32[]{:S(2)}) copy-start(bf16[64,1536]{1,0:T(8,128)(2,1)} %param.17) | copy-start | bytes 589828
  6.5 9.5 %copy-start.4 = (f32[12,64]{1,0:T(8,128)S(1)}, f32[12,64]{1,0:T(8,128)}, u32[]{:S(2)}) copy-start(f32[12,64]{1,0:T(8,128)} %param.23) | copy-start | bytes 9220
  9.7 6.8 %copy-start.5 = (f32[12,64]{1,0:T(8,128)S(1)}, f32[12,64]{1,0:T(8,128)}, u32[]{:S(2)}) copy-start(f32[12,64]{1,0:T(8,128)} %param.24) | copy-start | bytes 9220
  10.8 15.6 %all-to-all-start = ((bf16[8,24,1536]{2,1,0:T(8,128)(2,1)}), bf16[8,24,1536]{2,1,0:T(8,128)(2,1)S(1)}, u32[]{:S(2)}, u32[]{:S(2)}) async-start(bf16[8,24,1536]{2,1,0:T(8,128)(2,1)} %bitcast), calls=%async_computation | async-start | bytes 1179648 | tf_op jit(solution)/shard_map/all_to_all | solution.py:154
  16.0 54.7 %reduce-scatter.11.cloned.1.call-start = ((), (), s32[]{:S(2)}) async-start(), calls=%async_computation.9 | async-start | bytes 1966080 | tf_op jit(solution)/shard_map/reduce_scatter | solution.py:127
  35.9 78.8 %reduce-scatter.9.cloned.1.call-start = ((), (), s32[]{:S(2)}) async-start(), calls=%async_computation.8 | async-start | bytes 1966080 | tf_op jit(solution)/shard_map/reduce_scatter | solution.py:127
  45.6 113.9 %reduce-scatter.7.cloned.1.call-start = ((), (), s32[]{:S(2)}) async-start(), calls=%async_computation.7 | async-start | bytes 1966080 | tf_op jit(solution)/shard_map/reduce_scatter | solution.py:127
  55.1 149.9 %reduce-scatter.5.cloned.1.call-start = ((), (), s32[]{:S(2)}) async-start(), calls=%async_computation.6 | async-start | bytes 1966080 | tf_op jit(solution)/shard_map/reduce_scatter | solution.py:127
  64.6 0.7 copy-start.6
  233.1 7.3 %copy-start.3 = (s32[2]{0:T(128)S(1)}, s32[2]{0:T(128)}, u32[]{:S(2)}) copy-start(s32[2]{0:T(128)} %constant.39.clone.index_ref) | copy-start | bytes 28
  240.4 7.3 %copy-start.2 = (s32[2]{0:T(128)S(1)}, s32[2]{0:T(128)}, u32[]{:S(2)}) copy-start(s32[2]{0:T(128)} %constant.40.clone.index_ref) | copy-start | bytes 28
  247.8 22.5 %copy-start.1 = (bf16[64,1536]{1,0:T(8,128)(2,1)S(1)}, bf16[64,1536]{1,0:T(8,128)(2,1)}, u32[]{:S(2)}) copy-start(bf16[64,1536]{1,0:T(8,128)(2,1)} %param.17) | copy-start | bytes 589828
Sparse Core Ops, SparseCore 0:
  36.0 34.6 reduce-scatter.10
  73.0 41.6 reduce-scatter.8
  117.0 42.4 reduce-scatter.6
  161.7 43.2 reduce-scatter.4

commit v2 on v1

v2 whole, which is shorter than its diff:
```python
import functools

import jax
import jax.numpy as jnp
from jax import lax
from jax.experimental import pallas as pl
from jax.experimental.pallas import tpu as pltpu
from jax.sharding import PartitionSpec as P

EXPERTS = 8
BLOCK = 128
CAP = 24
UNITS = 8
CHAIN_UNITS = 8
LAG = 2
GROUP = 1


def widen(block_scale):
    return jnp.repeat(block_scale, BLOCK, axis=1).astype(jnp.bfloat16)


def spread(weights, scale_rows):
    depth = weights.shape[0]
    parts = [
        weights[k * BLOCK : (k + 1) * BLOCK, :] * scale_rows[k : k + 1, :]
        for k in range(depth // BLOCK)
    ]
    return jnp.concatenate(parts, axis=0) if len(parts) > 1 else parts[0]


def own_kernel(index_ref, x_ref, gate_ref, up_ref, gate_scale_ref, up_scale_ref, out_ref):
    @pl.when(index_ref[1] > 0)
    def _():
        x = x_ref[...]
        out_ref[0] = jnp.dot(
            x, spread(gate_ref[...], gate_scale_ref[...]), preferred_element_type=jnp.float32
        ).astype(jnp.bfloat16)
        out_ref[1] = jnp.dot(
            x, spread(up_ref[...], up_scale_ref[...]), preferred_element_type=jnp.float32
        ).astype(jnp.bfloat16)


def tile(width, most):
    return max(t for t in range(BLOCK, most + 1, BLOCK) if width % t == 0)


def own_terms(index, x, weights, count):
    w_gate, w_up, gate_scale, up_scale = weights
    rows, depth = x.shape
    width = own_tile(count)
    column = lambda j, index: (0, index[0] + jnp.where(index[1] > 0, j, 0))
    weight_spec = pl.BlockSpec((depth, width), column)
    scale_spec = pl.BlockSpec((depth // BLOCK, width), column)
    return pl.pallas_call(
        own_kernel,
        grid_spec=pltpu.PrefetchScalarGridSpec(
            num_scalar_prefetch=1,
            grid=(count // width,),
            in_specs=[
                pl.BlockSpec((rows, depth), lambda j, index: (0, 0)),
                weight_spec,
                weight_spec,
                scale_spec,
                scale_spec,
            ],
            out_specs=pl.BlockSpec((2, rows, width), lambda j, index: (0, 0, j)),
        ),
        out_shape=jax.ShapeDtypeStruct((2, rows, count), jnp.bfloat16),
        compiler_params=pltpu.CompilerParams(vmem_limit_bytes=32 * 1024 * 1024),
        cost_estimate=pl.CostEstimate(
            flops=4 * rows * depth * count, bytes_accessed=8 * depth * count, transcendentals=0
        ),
        name="gate_up",
    )(index, x, w_gate, w_up, gate_scale, up_scale)


def own_tile(count):
    return tile(count, 512)


def down_kernel(index_ref, hidden_ref, weight_ref, scale_ref, total_ref, out_ref, *, steps):
    step = pl.program_id(0)

    @pl.when(step == 0)
    def _():
        out_ref[...] = total_ref[...]

    @pl.when(index_ref[1, step // steps] > 0)
    def _():
        out_ref[...] += jnp.dot(
            hidden_ref[0],
            spread(weight_ref[...], scale_ref[0]),
            preferred_element_type=jnp.float32,
        )


def down_add(index, hidden, w_down, down_scale, total):
    count, rows, unit = hidden.shape
    width = w_down.shape[1]
    depth = tile(unit, 512)
    steps = unit // depth

    def at(j, index):
        slot = j // steps
        return index[0, slot] * steps + jnp.where(index[1, slot] > 0, j % steps, 0)

    scale = down_scale.reshape(-1, depth // BLOCK, width)
    return pl.pallas_call(
        functools.partial(down_kernel, steps=steps),
        grid_spec=pltpu.PrefetchScalarGridSpec(
            num_scalar_prefetch=1,
            grid=(count * steps,),
            in_specs=[
                pl.BlockSpec((1, rows, depth), lambda j, index: (j // steps, 0, j % steps)),
                pl.BlockSpec((depth, width), lambda j, index: (at(j, index), 0)),
                pl.BlockSpec((1, depth // BLOCK, width), lambda j, index: (at(j, index), 0, 0)),
                pl.BlockSpec((rows, width), lambda j, index: (0, 0)),
            ],
            out_specs=pl.BlockSpec((rows, width), lambda j, index: (0, 0)),
        ),
        out_shape=jax.ShapeDtypeStruct((rows, width), jnp.float32),
        input_output_aliases={4: 0},
        compiler_params=pltpu.CompilerParams(vmem_limit_bytes=32 * 1024 * 1024),
        cost_estimate=pl.CostEstimate(
            flops=2 * rows * width * unit * count,
            bytes_accessed=4 * width * unit * count,
            transcendentals=0,
        ),
        name="down",
    )(index, hidden, w_down, scale, total)


def activate(sums):
    gate, up = sums[0].astype(jnp.float32), sums[1].astype(jnp.float32)
    return (jax.nn.silu(gate) * up).astype(jnp.bfloat16)


def chain_pairs(stages, experts, moving):
    up, back = [], []
    for expert in range(experts):
        for place in moving:
            here, there = place * experts + expert, (place + 1) * experts + expert
            if expert % 2:
                here = (stages - 1 - place) * experts + expert
                there = (stages - 2 - place) * experts + expert
            up.append((here, there))
            back.append((there, here))
    return up, back


def after(value, *done):
    return lax.optimization_barrier((value, *done))[0]


def expert_rows(x, weights, w_down, down_scale):
    stages, experts = lax.axis_size("fsdp"), lax.axis_size("expert")
    hidden_width = weights[0].shape[1]
    unit = hidden_width // UNITS
    chain = CHAIN_UNITS if stages <= 4 else 0
    rest = hidden_width - chain * unit
    rows = x.shape[0]
    total = jnp.zeros((rows, w_down.shape[1]), jnp.float32)

    def call_part():
        index = jnp.array([chain * unit // own_tile(rest), 1], jnp.int32)
        own = own_terms(index, x, weights, rest)
        summed = lax.psum_scatter(own, "fsdp", scatter_dimension=1, tiled=True)
        return lax.all_gather(activate(summed), "fsdp", axis=0, tiled=True)

    def call_down(hidden, total):
        count = UNITS - chain
        stacked = jnp.stack([hidden[:, u * unit : (u + 1) * unit] for u in range(count)])
        index = jnp.array([list(range(chain, UNITS)), [1] * count], jnp.int32)
        return down_add(index, stacked, w_down, down_scale, total)

    if not chain:
        return call_down(call_part(), total)
    line, expert = lax.axis_index("fsdp"), lax.axis_index("expert")
    place = jnp.where(expert % 2 == 0, line, stages - 1 - line)
    last = stages - 1
    reach = LAG * last
    axes = ("fsdp", "expert")

    def own_at(slot, *done):
        held = slot - LAG * place
        counts = (held >= 0) & (held < chain)
        first = jnp.clip(held, 0, chain - 1) * (unit // own_tile(unit))
        index = jnp.stack([first, counts]).astype(jnp.int32)
        return own_terms(after(index, *done) if done else index, x, weights, unit)

    gathered = call_part() if rest else None
    sent, told = {}, {}
    group = []
    own = own_at(0)
    for slot in range(chain + 2 * reach):
        fresh = None
        token = own
        if slot < chain + reach:
            sums = own
            if slot - LAG in sent:
                sums = (
                    sums.astype(jnp.float32) + sent.pop(slot - LAG).astype(jnp.float32)
                ).astype(jnp.bfloat16)
            moving = [p for p in range(last) if 0 <= slot - LAG * p < chain]
            if moving:
                sent[slot] = lax.ppermute(sums, axes, chain_pairs(stages, experts, moving)[0])
            if slot >= reach:
                fresh = activate(sums)
            token = sums
            if slot + 1 < chain + reach:
                own = own_at(slot + 1, sums)
                token = own
        if slot < reach:
            continue
        arrived = told.pop(slot - LAG, None)
        hidden = arrived if fresh is None else fresh
        if fresh is not None and arrived is not None:
            hidden = jnp.where(place == last, after(fresh, token), arrived)
        moving = [p for p in range(last) if 0 <= slot - reach - LAG * (last - 1 - p) < chain]
        if moving:
            told[slot] = lax.ppermute(hidden, axes, chain_pairs(stages, experts, moving)[1])
        held = slot - reach - LAG * (last - place)
        counts = ((held >= 0) & (held < chain)).astype(jnp.int32)
        group.append((jnp.clip(held, 0, chain - 1), counts, hidden))
        if len(group) == GROUP or slot == chain + 2 * reach - 1:
            index = jnp.stack([jnp.stack([g[0] for g in group]), jnp.stack([g[1] for g in group])])
            total = down_add(
                index.astype(jnp.int32), jnp.stack([g[2] for g in group]), w_down, down_scale, total
            )
            group = []
            if slot + 1 < chain + reach:
                own = after(own, total)
            elif slot - LAG + 1 in told:
                told[slot - LAG + 1] = after(told[slot - LAG + 1], total)
    return total if gathered is None else call_down(gathered, total)


def shards(tokens, expert_ids, gate_values, w_gate, w_up, w_down, scale_gate, scale_up, scale_down):
    device_count = lax.axis_size("expert")
    slices = device_count // EXPERTS
    local_tokens = tokens.shape[0]
    feature_cols = tokens.shape[1]
    slot_total = EXPERTS * CAP
    flat_ids = expert_ids.reshape(-1)
    onehot = (flat_ids[:, None] == jnp.arange(EXPERTS, dtype=jnp.int32)[None, :]).astype(jnp.int32)
    slot_rank = jnp.sum((jnp.cumsum(onehot, axis=0) - onehot) * onehot, axis=1)
    target = flat_ids * CAP + slot_rank
    placing = (target[:, None] == jnp.arange(slot_total, dtype=jnp.int32)[None, :]).astype(
        jnp.float32
    )
    token_map = jnp.sum(placing.reshape(local_tokens, 2, slot_total), axis=1).astype(jnp.bfloat16)
    packed = jnp.einsum("ts,td->sd", token_map, tokens, preferred_element_type=jnp.float32).astype(
        jnp.bfloat16
    )
    outgoing = jnp.broadcast_to(
        packed.reshape(EXPERTS, 1, CAP, feature_cols), (EXPERTS, slices, CAP, feature_cols)
    ).reshape(device_count * CAP, feature_cols)
    incoming = lax.all_to_all(outgoing, "expert", split_axis=0, concat_axis=0, tiled=True)
    weights = (w_gate, w_up, widen(scale_gate), widen(scale_up))
    partial_rows = expert_rows(incoming, weights, w_down, widen(scale_down)).astype(jnp.bfloat16)
    returned = lax.all_to_all(partial_rows, "expert", split_axis=0, concat_axis=0, tiled=True)
    slice_sums = jnp.sum(
        returned.reshape(EXPERTS, slices, CAP, feature_cols).astype(jnp.float32), axis=1
    )
    slice_sums = slice_sums.reshape(slot_total, feature_cols)
    weights_map = jnp.sum(
        (placing * gate_values.reshape(-1)[:, None]).reshape(local_tokens, 2, slot_total), axis=1
    )
    mixed_rows = jnp.dot(
        weights_map, slice_sums, precision=lax.Precision.HIGHEST, preferred_element_type=jnp.float32
    )
    return mixed_rows.astype(jnp.bfloat16)


def solution(mesh):
    in_specs = (
        P("expert", "fsdp"),
        P("expert", None),
        P("expert", None),
        P("fsdp", "expert"),
        P("fsdp", "expert"),
        P("expert", "fsdp"),
        P("fsdp", "expert"),
        P("fsdp", "expert"),
        P("expert", "fsdp"),
    )
    out_specs = P("expert", "fsdp")
    return jax.shard_map(shards, mesh=mesh, in_specs=in_specs, out_specs=out_specs, check_vma=False)
```

time: 278 us -> 203 us (0.73)
  blocking collectives: 111 us -> 12.8 us
  starting transfers between devices: 5.33 us -> 40.6 us
  waiting for transfers between devices: 68 us -> 37.2 us
  Pallas kernels: 67.2 us -> 89.8 us
  between operations: 13.4 us -> 1 us
  other arithmetic: 6.55 us -> 15.9 us
    all_gather x4 -> x0, blocking collectives: 96.9 us -> none  [expert_rows(): lax.all_gather(activate(sums[c][0], sums[c][1]), 'fsdp', axis=0, tiled=True)]
    reduce_scatter x4 -> x0, waiting for transfers between devices: 58.4 us -> none  [expert_rows(): sums.append(lax.psum_scatter(own, 'fsdp', scatter_dimension=1, tiled=True))]
    ppermute x0 -> x24, starting transfers between devices: none -> 35.4 us  [the longest x12 22.2 us: expert_rows(): lax.ppermute(sums, axes, chain_pairs(stages, experts, moving)[0])]
    ppermute x0 -> x24, waiting for transfers between devices: none -> 28.4 us  [the longest x12 27.8 us: expert_rows(): lax.ppermute(hidden, axes, chain_pairs(stages, experts, moving)[1])]
    pallas_call x4 -> x14, Pallas kernels: 38 us -> 50.2 us  [own_terms(): pl.pallas_call(own_kernel, grid_spec=pltpu.PrefetchScalarGridSpec(num_sca...]
    pallas_call x4 -> x14, Pallas kernels: 29.2 us -> 39.7 us  [down_add(): pl.pallas_call(functools.partial(down_kernel, steps=steps), grid_spec=plt...]
    convert_element_type x1 -> x13, other arithmetic: 0.06 us -> 9.12 us  [the longest x12 9.06 us: expert_rows(): sums = (sums.astype(jnp.float32) + sent.pop(slot - LAG).astype(jnp.float3...]
  transfers between devices with their start and end apart: 5 -> 25, of which waited for: 5 -> 9; matrix products, arithmetic and copies ran while one was open for 2% -> 7% of each run, Pallas kernels for 10% -> 41%
where the time goes in v2:
time: 203 us; the launch traced here: 202 us
  Pallas kernels  89.8 us (44%)
  starting transfers between devices  40.6 us (20%)
  waiting for transfers between devices  37.2 us (18%)
  other arithmetic  15.9 us (8%)
  blocking collectives  12.8 us (6%)
  local copies, waits for them, and re-layouts  2.42 us (1%)
  matrix products  2.26 us (1%)
    pallas_call x14, Pallas kernels, own_terms(): pl.pallas_call(own_kernel, grid_spec=pltpu.PrefetchScalarGridSpec(num_sca...  50.2 us
    pallas_call x14, Pallas kernels, down_add(): pl.pallas_call(functools.partial(down_kernel, steps=steps), grid_spec=plt...  39.7 us
    ppermute x12, waiting for transfers between devices, expert_rows(): lax.ppermute(hidden, axes, chain_pairs(stages, experts, moving)[1])  27.8 us
    ppermute x12, starting transfers between devices, expert_rows(): lax.ppermute(sums, axes, chain_pairs(stages, experts, moving)[0])  22.2 us
    ppermute x12, starting transfers between devices, expert_rows(): lax.ppermute(hidden, axes, chain_pairs(stages, experts, moving)[1])  13.3 us
    all_to_all x1, blocking collectives, shards(): lax.all_to_all(partial_rows, 'expert', split_axis=0, concat_axis=0, tiled...  12.8 us
    convert_element_type x12, other arithmetic, expert_rows(): sums = (sums.astype(jnp.float32) + sent.pop(slot - LAG).astype(jnp.float3...  9.06 us
    all_to_all x1, waiting for transfers between devices, shards(): lax.all_to_all(outgoing, 'expert', split_axis=0, concat_axis=0, tiled=True)  8.79 us
  transfers between devices with their start and end apart: 25, of which 9 were waited for; matrix products, arithmetic and copies ran while one was open for 7% of the time, Pallas kernels for 41%

profile of v2, /device:TPU:0, one launch (start us, length us, event | category | flops | bytes accessed | tf_op | source)
XLA Modules:
  0.0 202.0 jit_solution(15854115332301291762)
XLA Ops:
  4.9 5.2 %all-to-all-start = ((bf16[8,24,1536]{2,1,0:T(8,128)(2,1)}), bf16[8,24,1536]{2,1,0:T(8,128)(2,1)S(1)}, u32[]{:S(2)}, u32[]{:S(2)}) async-start(bf16[8,24,1536]{2,1,0:T(8,128)(2,1)} %bitcast.30), calls=%async_computation | async-start | bytes 1179648 | tf_op jit(solution)/shard_map/all_to_all | solution.py:259
  11.7 8.8 %all-to-all-done = bf16[8,24,1536]{2,1,0:T(8,128)(2,1)S(1)} async-done(((bf16[8,24,1536]{2,1,0:T(8,128)(2,1)}), bf16[8,24,1536]{2,1,0:T(8,128)(2,1)S(1)}, u32[]{:S(2)}, u32[]{:S(2)}) %all-to-all-start) | async-done | bytes 589856 | tf_op jit(solution)/shard_map/all_to_all | solution.py:259
  20.5 4.3 %gate_up.14 = bf16[2,192,1024]{2,1,0:T(8,128)(2,1)S(1)} custom-call(s32[2]{0:T(128)S(1)} %pad_add_fusion.27.index_ref, bf16[192,1536]{1,0:T(8,128)(2,1)S(1)} %bitcast.186, bf16[1536,8192]{1,0:T(8,128)(2,1)} %gate_ref.27, bf16[1536,8192]{1,0:T(8,128)(2,1)} %up_ref.27, bf16[12,8192]{1,0:T(8,128)(2,1)S(1)} %bitcast.200, bf16[12,8192]{1,0:T(8,128)(2,1)S(1)} %bitcast.214), custom_call_target="tpu_custom_call" | custom-call | flops 1207959552 | bytes 12582912 | tf_op jit(solution)/shard_map/gate_up/pallas_call | solution.py:55
  26.9 4.3 %gate_up.15 = bf16[2,192,1024]{2,1,0:T(8,128)(2,1)S(1)} custom-call(s32[2]{0:T(128)S(1)} %pad_add_fusion.26.index_ref, bf16[192,1536]{1,0:T(8,128)(2,1)S(1)} %bitcast.187, bf16[1536,8192]{1,0:T(8,128)(2,1)} %gate_ref.27, bf16[1536,8192]{1,0:T(8,128)(2,1)} %up_ref.27, bf16[12,8192]{1,0:T(8,128)(2,1)S(1)} %bitcast.201, bf16[12,8192]{1,0:T(8,128)(2,1)S(1)} %bitcast.215), custom_call_target="tpu_custom_call" | custom-call | flops 1207959552 | bytes 12582912 | tf_op jit(solution)/shard_map/gate_up/pallas_call | solution.py:55
  33.4 4.3 %gate_up.16 = bf16[2,192,1024]{2,1,0:T(8,128)(2,1)S(1)} custom-call(s32[2]{0:T(128)S(1)} %pad_add_fusion.25.index_ref, bf16[192,1536]{1,0:T(8,128)(2,1)S(1)} %bitcast.188, bf16[1536,8192]{1,0:T(8,128)(2,1)} %gate_ref.27, bf16[1536,8192]{1,0:T(8,128)(2,1)} %up_ref.27, bf16[12,8192]{1,0:T(8,128)(2,1)S(1)} %bitcast.202, bf16[12,8192]{1,0:T(8,128)(2,1)S(1)} %bitcast.216), custom_call_target="tpu_custom_call" | custom-call | flops 1207959552 | bytes 12582912 | tf_op jit(solution)/shard_map/gate_up/pallas_call | solution.py:55
  38.0 3.7 %collective-permute-start.2 = (bf16[2,192,1024]{2,1,0:T(8,128)(2,1)S(1)}, bf16[2,192,1024]{2,1,0:T(8,128)(2,1)}, u32[]{:S(2)}, u32[]{:S(2)}) collective-permute-start(bf16[2,192,1024]{2,1,0:T(8,128)(2,1)S(1)} %add_convert_fusion.11), channel_id=1, source_target_pairs={{0,8},{8,16},{25,17},{17,9},{2,10},{10,18},{27,19},{19,11},{4,12},... | collective-permute-start | bytes 2359304 | tf_op jit(solution)/shard_map/ppermute | solution.py:207
  41.8 4.3 %gate_up.17 = bf16[2,192,1024]{2,1,0:T(8,128)(2,1)S(1)} custom-call(s32[2]{0:T(128)S(1)} %pad_add_fusion.24.index_ref, bf16[192,1536]{1,0:T(8,128)(2,1)S(1)} %bitcast.189, bf16[1536,8192]{1,0:T(8,128)(2,1)} %gate_ref.27, bf16[1536,8192]{1,0:T(8,128)(2,1)} %up_ref.27, bf16[12,8192]{1,0:T(8,128)(2,1)S(1)} %bitcast.203, bf16[12,8192]{1,0:T(8,128)(2,1)S(1)} %bitcast.217), custom_call_target="tpu_custom_call" | custom-call | flops 1207959552 | bytes 12582912 | tf_op jit(solution)/shard_map/gate_up/pallas_call | solution.py:55
  48.4 3.8 %collective-permute-start.3 = (bf16[2,192,1024]{2,1,0:T(8,128)(2,1)}, bf16[2,192,1024]{2,1,0:T(8,128)(2,1)}, u32[]{:S(2)}, u32[]{:S(2)}) collective-permute-start(bf16[2,192,1024]{2,1,0:T(8,128)(2,1)} %add_convert_fusion.10), channel_id=1, source_target_pairs={{0,8},{8,16},{25,17},{17,9},{2,10},{10,18},{27,19},{19,11},{4,12},... | collective-permute-start | bytes 2359304 | tf_op jit(solution)/shard_map/ppermute | solution.py:207
  52.3 4.3 %gate_up.18 = bf16[2,192,1024]{2,1,0:T(8,128)(2,1)S(1)} custom-call(s32[2]{0:T(128)S(1)} %pad_add_fusion.23.index_ref, bf16[192,1536]{1,0:T(8,128)(2,1)S(1)} %bitcast.190, bf16[1536,8192]{1,0:T(8,128)(2,1)} %gate_ref.27, bf16[1536,8192]{1,0:T(8,128)(2,1)} %up_ref.27, bf16[12,8192]{1,0:T(8,128)(2,1)S(1)} %bitcast.204, bf16[12,8192]{1,0:T(8,128)(2,1)S(1)} %bitcast.218), custom_call_target="tpu_custom_call" | custom-call | flops 1207959552 | bytes 12582912 | tf_op jit(solution)/shard_map/gate_up/pallas_call | solution.py:55
  60.7 4.3 %gate_up.19 = bf16[2,192,1024]{2,1,0:T(8,128)(2,1)S(1)} custom-call(s32[2]{0:T(128)S(1)} %pad_add_fusion.22.index_ref, bf16[192,1536]{1,0:T(8,128)(2,1)S(1)} %bitcast.191, bf16[1536,8192]{1,0:T(8,128)(2,1)} %gate_ref.27, bf16[1536,8192]{1,0:T(8,128)(2,1)} %up_ref.27, bf16[12,8192]{1,0:T(8,128)(2,1)S(1)} %bitcast.205, bf16[12,8192]{1,0:T(8,128)(2,1)S(1)} %bitcast.219), custom_call_target="tpu_custom_call" | custom-call | flops 1207959552 | bytes 12582912 | tf_op jit(solution)/shard_map/gate_up/pallas_call | solution.py:55
  67.9 4.3 %gate_up.20 = bf16[2,192,1024]{2,1,0:T(8,128)(2,1)S(1)} custom-call(s32[2]{0:T(128)S(1)} %pad_add_fusion.21.index_ref, bf16[192,1536]{1,0:T(8,128)(2,1)S(1)} %bitcast.192, bf16[1536,8192]{1,0:T(8,128)(2,1)} %gate_ref.27, bf16[1536,8192]{1,0:T(8,128)(2,1)} %up_ref.27, bf16[12,8192]{1,0:T(8,128)(2,1)S(1)} %bitcast.206, bf16[12,8192]{1,0:T(8,128)(2,1)S(1)} %bitcast.220), custom_call_target="tpu_custom_call" | custom-call | flops 1207959552 | bytes 12582912 | tf_op jit(solution)/shard_map/gate_up/pallas_call | solution.py:55
  78.5 4.3 %gate_up.21 = bf16[2,192,1024]{2,1,0:T(8,128)(2,1)S(1)} custom-call(s32[2]{0:T(128)S(1)} %pad_add_fusion.20.index_ref, bf16[192,1536]{1,0:T(8,128)(2,1)S(1)} %bitcast.193, bf16[1536,8192]{1,0:T(8,128)(2,1)} %gate_ref.27, bf16[1536,8192]{1,0:T(8,128)(2,1)} %up_ref.27, bf16[12,8192]{1,0:T(8,128)(2,1)S(1)} %bitcast.207, bf16[12,8192]{1,0:T(8,128)(2,1)S(1)} %bitcast.221), custom_call_target="tpu_custom_call" | custom-call | flops 1207959552 | bytes 12582912 | tf_op jit(solution)/shard_map/gate_up/pallas_call | solution.py:55
  125.5 8.9 %collective-permute-done.15 = bf16[192,1024]{1,0:T(8,128)(2,1)S(1)} collective-permute-done((bf16[192,1024]{1,0:T(8,128)(2,1)S(1)}, bf16[192,1024]{1,0:T(8,128)(2,1)S(1)}, u32[]{:S(2)}, u32[]{:S(2)}) %collective-permute-start.15) | collective-permute-done | bytes 393248 | tf_op jit(solution)/shard_map/ppermute | solution.py:222
  135.8 3.2 %down.20.total_ref = f32[192,1536]{1,0:T(8,128)S(1)} custom-call(s32[2,1]{1,0:T(2,128)S(1)} %pad_add_fusion.7.index_ref, bf16[1,192,1024]{2,1,0:T(8,128)(2,1)S(1)} %bitcast.228, bf16[8192,1536]{1,0:T(8,128)(2,1)} %weight_ref.27, bf16[16,4,1536]{2,1,0:T(4,128)(2,1)S(1)} %convert_element_type.339.scale_ref, ...), custom_call_target="tpu_custom_call", output_to_operand_aliasing={{}: (4, {})} | custom-call | flops 603979776 | bytes 6291456 | tf_op jit(solution)/shard_map/down/pallas_call | solution.py:109
  139.6 4.0 %collective-permute-done.17 = bf16[192,1024]{1,0:T(8,128)(2,1)S(1)} collective-permute-done((bf16[192,1024]{1,0:T(8,128)(2,1)S(1)}, bf16[192,1024]{1,0:T(8,128)(2,1)S(1)}, u32[]{:S(2)}, u32[]{:S(2)}) %collective-permute-start.17) | collective-permute-done | bytes 393248 | tf_op jit(solution)/shard_map/ppermute | solution.py:222
  145.0 3.2 %down.21.total_ref = f32[192,1536]{1,0:T(8,128)S(1)} custom-call(s32[2,1]{1,0:T(2,128)S(1)} %pad_add_fusion.9.index_ref, bf16[1,192,1024]{2,1,0:T(8,128)(2,1)S(1)} %bitcast.232, bf16[8192,1536]{1,0:T(8,128)(2,1)} %weight_ref.27, bf16[16,4,1536]{2,1,0:T(4,128)(2,1)S(1)} %convert_element_type.339.scale_ref, ...), custom_call_target="tpu_custom_call", output_to_operand_aliasing={{}: (4, {})} | custom-call | flops 603979776 | bytes 6291456 | tf_op jit(solution)/shard_map/down/pallas_call | solution.py:109
  148.3 4.1 %collective-permute-done.19 = bf16[192,1024]{1,0:T(8,128)(2,1)S(1)} collective-permute-done((bf16[192,1024]{1,0:T(8,128)(2,1)S(1)}, bf16[192,1024]{1,0:T(8,128)(2,1)S(1)}, u32[]{:S(2)}, u32[]{:S(2)}) %collective-permute-start.19) | collective-permute-done | bytes 393248 | tf_op jit(solution)/shard_map/ppermute | solution.py:222
  153.7 3.2 %down.22.total_ref = f32[192,1536]{1,0:T(8,128)S(1)} custom-call(s32[2,1]{1,0:T(2,128)S(1)} %pad_add_fusion.8.index_ref, bf16[1,192,1024]{2,1,0:T(8,128)(2,1)S(1)} %bitcast.234, bf16[8192,1536]{1,0:T(8,128)(2,1)} %weight_ref.27, bf16[16,4,1536]{2,1,0:T(4,128)(2,1)S(1)} %convert_element_type.339.scale_ref, ...), custom_call_target="tpu_custom_call", output_to_operand_aliasing={{}: (4, {})} | custom-call | flops 603979776 | bytes 6291456 | tf_op jit(solution)/shard_map/down/pallas_call | solution.py:109
  156.9 3.7 %collective-permute-done.18 = bf16[192,1024]{1,0:T(8,128)(2,1)S(1)} collective-permute-done((bf16[192,1024]{1,0:T(8,128)(2,1)S(1)}, bf16[192,1024]{1,0:T(8,128)(2,1)S(1)}, u32[]{:S(2)}, u32[]{:S(2)}) %collective-permute-start.18) | collective-permute-done | bytes 393248 | tf_op jit(solution)/shard_map/ppermute | solution.py:222
  165.2 4.0 %collective-permute-done.21 = bf16[192,1024]{1,0:T(8,128)(2,1)S(1)} collective-permute-done((bf16[192,1024]{1,0:T(8,128)(2,1)S(1)}, bf16[192,1024]{1,0:T(8,128)(2,1)S(1)}, u32[]{:S(2)}, u32[]{:S(2)}) %collective-permute-start.21) | collective-permute-done | bytes 393248 | tf_op jit(solution)/shard_map/ppermute | solution.py:222
  176.4 3.2 %down.25.total_ref = f32[192,1536]{1,0:T(8,128)S(1)} custom-call(s32[2,1]{1,0:T(2,128)S(1)} %pad_add_fusion.13.index_ref, bf16[1,192,1024]{2,1,0:T(8,128)(2,1)S(1)} %bitcast.236, bf16[8192,1536]{1,0:T(8,128)(2,1)} %weight_ref.27, bf16[16,4,1536]{2,1,0:T(4,128)(2,1)S(1)} %convert_element_type.339.scale_ref, ...), custom_call_target="tpu_custom_call", output_to_operand_aliasing={{}: (4, {})} | custom-call | flops 603979776 | bytes 6291456 | tf_op jit(solution)/shard_map/down/pallas_call | solution.py:109
  179.7 3.2 %down.26.total_ref = f32[192,1536]{1,0:T(8,128)S(1)} custom-call(s32[2,1]{1,0:T(2,128)S(1)} %pad_add_fusion.12.index_ref, bf16[1,192,1024]{2,1,0:T(8,128)(2,1)S(1)} %bitcast.238, bf16[8192,1536]{1,0:T(8,128)(2,1)} %weight_ref.27, bf16[16,4,1536]{2,1,0:T(4,128)(2,1)S(1)} %convert_element_type.339.scale_ref, ...), custom_call_target="tpu_custom_call", output_to_operand_aliasing={{}: (4, {})} | custom-call | flops 603979776 | bytes 6291456 | tf_op jit(solution)/shard_map/down/pallas_call | solution.py:109
  184.7 3.2 %down.27 = f32[192,1536]{1,0:T(8,128)S(1)} custom-call(s32[2,1]{1,0:T(2,128)S(1)} %pad_add_fusion.index_ref, bf16[1,192,1024]{2,1,0:T(8,128)(2,1)S(1)} %bitcast.239, bf16[8192,1536]{1,0:T(8,128)(2,1)} %weight_ref.27, bf16[16,4,1536]{2,1,0:T(4,128)(2,1)S(1)} %convert_element_type.339.scale_ref, ...), custom_call_target="tpu_custom_call", output_to_operand_aliasing={{}: (4, {})} | custom-call | flops 603979776 | bytes 6291456 | tf_op jit(solution)/shard_map/down/pallas_call | solution.py:109
  188.1 12.8 %all_to_all.23 = bf16[8,24,1536]{2,1,0:T(8,128)(2,1)S(1)} all-to-all(bf16[8,24,1536]{2,1,0:T(8,128)(2,1)S(1)} %bitcast.240), channel_id=1, replica_groups=mesh['fsdp'=4,'expert'=8] {'expert'}, dimensions={0} | all-to-all | bytes 1179648 | tf_op jit(solution)/shard_map/all_to_all | solution.py:262
  (148 shorter events, 88.1 us)
Async XLA Ops:
  4.9 15.6 %all-to-all-start = ((bf16[8,24,1536]{2,1,0:T(8,128)(2,1)}), bf16[8,24,1536]{2,1,0:T(8,128)(2,1)S(1)}, u32[]{:S(2)}, u32[]{:S(2)}) async-start(bf16[8,24,1536]{2,1,0:T(8,128)(2,1)} %bitcast.30), calls=%async_computation | async-start | bytes 1179648 | tf_op jit(solution)/shard_map/all_to_all | solution.py:259
  24.8 12.9 %collective-permute-start = (bf16[2,192,1024]{2,1,0:T(8,128)(2,1)S(1)}, bf16[2,192,1024]{2,1,0:T(8,128)(2,1)S(1)}, u32[]{:S(2)}, u32[]{:S(2)}) collective-permute-start(bf16[2,192,1024]{2,1,0:T(8,128)(2,1)S(1)} %gate_up.14), channel_id=1, source_target_pairs={{0,8},{25,17},{2,10},{27,19},{4,12},{29,21},{6,14},{31,23}} | collective-permute-start | bytes 2359304 | tf_op jit(solution)/shard_map/ppermute | solution.py:207
  31.2 14.9 %collective-permute-start.1 = (bf16[2,192,1024]{2,1,0:T(8,128)(2,1)S(1)}, bf16[2,192,1024]{2,1,0:T(8,128)(2,1)}, u32[]{:S(2)}, u32[]{:S(2)}) collective-permute-start(bf16[2,192,1024]{2,1,0:T(8,128)(2,1)S(1)} %gate_up.15), channel_id=1, source_target_pairs={{0,8},{25,17},{2,10},{27,19},{4,12},{29,21},{6,14},{31,23}} | collective-permute-start | bytes 2359304 | tf_op jit(solution)/shard_map/ppermute | solution.py:207
  38.0 18.6 %collective-permute-start.2 = (bf16[2,192,1024]{2,1,0:T(8,128)(2,1)S(1)}, bf16[2,192,1024]{2,1,0:T(8,128)(2,1)}, u32[]{:S(2)}, u32[]{:S(2)}) collective-permute-start(bf16[2,192,1024]{2,1,0:T(8,128)(2,1)S(1)} %add_convert_fusion.11), channel_id=1, source_target_pairs={{0,8},{8,16},{25,17},{17,9},{2,10},{10,18},{27,19},{19,11},{4,12},... | collective-permute-start | bytes 2359304 | tf_op jit(solution)/shard_map/ppermute | solution.py:207
  48.4 16.6 %collective-permute-start.3 = (bf16[2,192,1024]{2,1,0:T(8,128)(2,1)}, bf16[2,192,1024]{2,1,0:T(8,128)(2,1)}, u32[]{:S(2)}, u32[]{:S(2)}) collective-permute-start(bf16[2,192,1024]{2,1,0:T(8,128)(2,1)} %add_convert_fusion.10), channel_id=1, source_target_pairs={{0,8},{8,16},{25,17},{17,9},{2,10},{10,18},{27,19},{19,11},{4,12},... | collective-permute-start | bytes 2359304 | tf_op jit(solution)/shard_map/ppermute | solution.py:207
  58.0 14.1 %collective-permute-start.4 = (bf16[2,192,1024]{2,1,0:T(8,128)(2,1)S(1)}, bf16[2,192,1024]{2,1,0:T(8,128)(2,1)}, u32[]{:S(2)}, u32[]{:S(2)}) collective-permute-start(bf16[2,192,1024]{2,1,0:T(8,128)(2,1)S(1)} %add_convert_fusion.9), channel_id=1, source_target_pairs={{0,8},{8,16},{16,24},{25,17},{17,9},{9,1},{2,10},{10,18},{18,26},{... | collective-permute-start | bytes 2359304 | tf_op jit(solution)/shard_map/ppermute | solution.py:207
  66.5 16.3 %collective-permute-start.5 = (bf16[2,192,1024]{2,1,0:T(8,128)(2,1)S(1)}, bf16[2,192,1024]{2,1,0:T(8,128)(2,1)S(1)}, u32[]{:S(2)}, u32[]{:S(2)}) collective-permute-start(bf16[2,192,1024]{2,1,0:T(8,128)(2,1)S(1)} %add_convert_fusion.8), channel_id=1, source_target_pairs={{0,8},{8,16},{16,24},{25,17},{17,9},{9,1},{2,10},{10,18},{18,26},{... | collective-permute-start | bytes 2359304 | tf_op jit(solution)/shard_map/ppermute | solution.py:207
  73.6 18.7 %collective-permute-start.6 = (bf16[2,192,1024]{2,1,0:T(8,128)(2,1)S(1)}, bf16[2,192,1024]{2,1,0:T(8,128)(2,1)S(1)}, u32[]{:S(2)}, u32[]{:S(2)}) collective-permute-start(bf16[2,192,1024]{2,1,0:T(8,128)(2,1)S(1)} %add_convert_fusion.7), channel_id=1, source_target_pairs={{0,8},{8,16},{16,24},{25,17},{17,9},{9,1},{2,10},{10,18},{18,26},{... | collective-permute-start | bytes 2359304 | tf_op jit(solution)/shard_map/ppermute | solution.py:207
  83.1 16.8 %collective-permute-start.8 = (bf16[2,192,1024]{2,1,0:T(8,128)(2,1)S(1)}, bf16[2,192,1024]{2,1,0:T(8,128)(2,1)S(1)}, u32[]{:S(2)}, u32[]{:S(2)}) collective-permute-start(bf16[2,192,1024]{2,1,0:T(8,128)(2,1)S(1)} %add_convert_fusion.6), channel_id=1, source_target_pairs={{0,8},{8,16},{16,24},{25,17},{17,9},{9,1},{2,10},{10,18},{18,26},{... | collective-permute-start | bytes 2359304 | tf_op jit(solution)/shard_map/ppermute | solution.py:207
  91.7 12.2 %collective-permute-start.9 = (bf16[192,1024]{1,0:T(8,128)(2,1)S(1)}, bf16[192,1024]{1,0:T(8,128)(2,1)S(1)}, u32[]{:S(2)}, u32[]{:S(2)}) collective-permute-start(bf16[192,1024]{1,0:T(8,128)(2,1)S(1)} %fusion.9), channel_id=1, source_target_pairs={{24,16},{1,9},{26,18},{3,11},{28,20},{5,13},{30,22},{7,15}} | collective-permute-start | bytes 1179656 | tf_op jit(solution)/shard_map/ppermute | solution.py:222
  92.7 14.2 %collective-permute-start.10 = (bf16[2,192,1024]{2,1,0:T(8,128)(2,1)S(1)}, bf16[2,192,1024]{2,1,0:T(8,128)(2,1)S(1)}, u32[]{:S(2)}, u32[]{:S(2)}) collective-permute-start(bf16[2,192,1024]{2,1,0:T(8,128)(2,1)S(1)} %add_convert_fusion.5), channel_id=1, source_target_pairs={{8,16},{16,24},{17,9},{9,1},{10,18},{18,26},{19,11},{11,3},{12,20}... | collective-permute-start | bytes 2359304 | tf_op jit(solution)/shard_map/ppermute | solution.py:207
  96.4 14.5 %collective-permute-start.11 = (bf16[192,1024]{1,0:T(8,128)(2,1)S(1)}, bf16[192,1024]{1,0:T(8,128)(2,1)S(1)}, u32[]{:S(2)}, u32[]{:S(2)}) collective-permute-start(bf16[192,1024]{1,0:T(8,128)(2,1)S(1)} %broadcast_select_fusion.5), channel_id=1, source_target_pairs={{16,8},{24,16},{9,17},{1,9},{18,10},{26,18},{11,19},{3,11},{20,12}... | collective-permute-start | bytes 1179656 | tf_op jit(solution)/shard_map/ppermute | solution.py:222
  100.2 14.3 %collective-permute-start.12 = (bf16[2,192,1024]{2,1,0:T(8,128)(2,1)S(1)}, bf16[2,192,1024]{2,1,0:T(8,128)(2,1)S(1)}, u32[]{:S(2)}, u32[]{:S(2)}) collective-permute-start(bf16[2,192,1024]{2,1,0:T(8,128)(2,1)S(1)} %add_convert_fusion.4), channel_id=1, source_target_pairs={{8,16},{16,24},{17,9},{9,1},{10,18},{18,26},{19,11},{11,3},{12,20}... | collective-permute-start | bytes 2359304 | tf_op jit(solution)/shard_map/ppermute | solution.py:207
  103.9 14.5 %collective-permute-start.13 = (bf16[192,1024]{1,0:T(8,128)(2,1)S(1)}, bf16[192,1024]{1,0:T(8,128)(2,1)S(1)}, u32[]{:S(2)}, u32[]{:S(2)}) collective-permute-start(bf16[192,1024]{1,0:T(8,128)(2,1)S(1)} %broadcast_select_fusion.4), channel_id=1, source_target_pairs={{16,8},{24,16},{9,17},{1,9},{18,10},{26,18},{11,19},{3,11},{20,12}... | collective-permute-start | bytes 1179656 | tf_op jit(solution)/shard_map/ppermute | solution.py:222
  107.2 15.1 %collective-permute-start.14 = (bf16[2,192,1024]{2,1,0:T(8,128)(2,1)S(1)}, bf16[2,192,1024]{2,1,0:T(8,128)(2,1)S(1)}, u32[]{:S(2)}, u32[]{:S(2)}) collective-permute-start(bf16[2,192,1024]{2,1,0:T(8,128)(2,1)S(1)} %add_convert_fusion.3), channel_id=1, source_target_pairs={{16,24},{9,1},{18,26},{11,3},{20,28},{13,5},{22,30},{15,7}} | collective-permute-start | bytes 2359304 | tf_op jit(solution)/shard_map/ppermute | solution.py:207
  110.9 23.5 %collective-permute-start.15 = (bf16[192,1024]{1,0:T(8,128)(2,1)S(1)}, bf16[192,1024]{1,0:T(8,128)(2,1)S(1)}, u32[]{:S(2)}, u32[]{:S(2)}) collective-permute-start(bf16[192,1024]{1,0:T(8,128)(2,1)S(1)} %broadcast_select_fusion.3), channel_id=1, source_target_pairs={{8,0},{16,8},{24,16},{17,25},{9,17},{1,9},{10,2},{18,10},{26,18},{... | collective-permute-start | bytes 1179656 | tf_op jit(solution)/shard_map/ppermute | solution.py:222
  114.8 24.2 %collective-permute-start.16 = (bf16[2,192,1024]{2,1,0:T(8,128)(2,1)S(1)}, bf16[2,192,1024]{2,1,0:T(8,128)(2,1)S(1)}, u32[]{:S(2)}, u32[]{:S(2)}) collective-permute-start(bf16[2,192,1024]{2,1,0:T(8,128)(2,1)S(1)} %add_convert_fusion.2), channel_id=1, source_target_pairs={{16,24},{9,1},{18,26},{11,3},{20,28},{13,5},{22,30},{15,7}} | collective-permute-start | bytes 2359304 | tf_op jit(solution)/shard_map/ppermute | solution.py:207
  118.5 25.1 %collective-permute-start.17 = (bf16[192,1024]{1,0:T(8,128)(2,1)S(1)}, bf16[192,1024]{1,0:T(8,128)(2,1)S(1)}, u32[]{:S(2)}, u32[]{:S(2)}) collective-permute-start(bf16[192,1024]{1,0:T(8,128)(2,1)S(1)} %broadcast_select_fusion.2), channel_id=1, source_target_pairs={{8,0},{16,8},{24,16},{17,25},{9,17},{1,9},{10,2},{18,10},{26,18},{... | collective-permute-start | bytes 1179656 | tf_op jit(solution)/shard_map/ppermute | solution.py:222
  134.5 17.9 %collective-permute-start.19 = (bf16[192,1024]{1,0:T(8,128)(2,1)S(1)}, bf16[192,1024]{1,0:T(8,128)(2,1)S(1)}, u32[]{:S(2)}, u32[]{:S(2)}) collective-permute-start(bf16[192,1024]{1,0:T(8,128)(2,1)S(1)} %broadcast_select_fusion.1), channel_id=1, source_target_pairs={{8,0},{16,8},{24,16},{17,25},{9,17},{1,9},{10,2},{18,10},{26,18},{... | collective-permute-start | bytes 1179656 | tf_op jit(solution)/shard_map/ppermute | solution.py:222
  143.7 16.9 %collective-permute-start.18 = (bf16[192,1024]{1,0:T(8,128)(2,1)S(1)}, bf16[192,1024]{1,0:T(8,128)(2,1)S(1)}, u32[]{:S(2)}, u32[]{:S(2)}) collective-permute-start(bf16[192,1024]{1,0:T(8,128)(2,1)S(1)} %broadcast_select_fusion), channel_id=1, source_target_pairs={{8,0},{16,8},{24,16},{17,25},{9,17},{1,9},{10,2},{18,10},{26,18},{... | collective-permute-start | bytes 1179656 | tf_op jit(solution)/shard_map/ppermute | solution.py:222
  152.4 16.8 %collective-permute-start.21 = (bf16[192,1024]{1,0:T(8,128)(2,1)S(1)}, bf16[192,1024]{1,0:T(8,128)(2,1)S(1)}, u32[]{:S(2)}, u32[]{:S(2)}) collective-permute-start(bf16[192,1024]{1,0:T(8,128)(2,1)S(1)} %collective-permute-done.19), channel_id=1, source_target_pairs={{8,0},{16,8},{17,25},{9,17},{10,2},{18,10},{19,27},{11,19},{12,4},... | collective-permute-start | bytes 1179656 | tf_op jit(solution)/shard_map/ppermute | solution.py:222
  160.6 14.5 %collective-permute-start.20 = (bf16[192,1024]{1,0:T(8,128)(2,1)S(1)}, bf16[192,1024]{1,0:T(8,128)(2,1)S(1)}, u32[]{:S(2)}, u32[]{:S(2)}) collective-permute-start(bf16[192,1024]{1,0:T(8,128)(2,1)S(1)} %collective-permute-done.18), channel_id=1, source_target_pairs={{8,0},{16,8},{17,25},{9,17},{10,2},{18,10},{19,27},{11,19},{12,4},... | collective-permute-start | bytes 1179656 | tf_op jit(solution)/shard_map/ppermute | solution.py:222
  169.2 10.5 %collective-permute-start.23 = (bf16[192,1024]{1,0:T(8,128)(2,1)S(1)}, bf16[192,1024]{1,0:T(8,128)(2,1)S(1)}, u32[]{:S(2)}, u32[]{:S(2)}) collective-permute-start(bf16[192,1024]{1,0:T(8,128)(2,1)S(1)} %collective-permute-done.21), channel_id=1, source_target_pairs={{8,0},{17,25},{10,2},{19,27},{12,4},{21,29},{14,6},{23,31}} | collective-permute-start | bytes 1179656 | tf_op jit(solution)/shard_map/ppermute | solution.py:222
  175.1 9.7 %collective-permute-start.22 = (bf16[192,1024]{1,0:T(8,128)(2,1)S(1)}, bf16[192,1024]{1,0:T(8,128)(2,1)S(1)}, u32[]{:S(2)}, u32[]{:S(2)}) collective-permute-start(bf16[192,1024]{1,0:T(8,128)(2,1)S(1)} %collective-permute-done.20), channel_id=1, source_target_pairs={{8,0},{17,25},{10,2},{19,27},{12,4},{21,29},{14,6},{23,31}} | collective-permute-start | bytes 1179656 | tf_op jit(solution)/shard_map/ppermute | solution.py:222
  (7 other events, 60.0 us)

commit v3 on v2

--- a/solution.py
+++ b/solution.py
@@ -13,6 +13,7 @@
 UNITS = 8
 CHAIN_UNITS = 8
 LAG = 2
+HOLD = 2
 GROUP = 1
 
 
@@ -69,7 +70,7 @@
         out_shape=jax.ShapeDtypeStruct((2, rows, count), jnp.bfloat16),
         compiler_params=pltpu.CompilerParams(vmem_limit_bytes=32 * 1024 * 1024),
         cost_estimate=pl.CostEstimate(
-            flops=4 * rows * depth * count, bytes_accessed=8 * depth * count, transcendentals=0
+            flops=rows * depth * count // 8, bytes_accessed=depth * count // 8, transcendentals=0
         ),
         name="gate_up",
     )(index, x, w_gate, w_up, gate_scale, up_scale)
@@ -123,8 +124,8 @@
         input_output_aliases={4: 0},
         compiler_params=pltpu.CompilerParams(vmem_limit_bytes=32 * 1024 * 1024),
         cost_estimate=pl.CostEstimate(
-            flops=2 * rows * width * unit * count,
-            bytes_accessed=4 * width * unit * count,
+            flops=rows * width * unit * count // 16,
+            bytes_accessed=width * unit * count // 16,
             transcendentals=0,
         ),
         name="down",
@@ -189,50 +190,54 @@
         index = jnp.stack([first, counts]).astype(jnp.int32)
         return own_terms(after(index, *done) if done else index, x, weights, unit)
 
+    def hidden_of(number):
+        chosen = None
+        for p in range(stages):
+            value = held[number + begin + LAG * (last - p)]
+            chosen = value if chosen is None else jnp.where(place == p, value, chosen)
+        return chosen
+
     gathered = call_part() if rest else None
-    sent, told = {}, {}
-    group = []
+    begin = reach + HOLD
+    sent, fresh, held, told = {}, {}, {}, {}
     own = own_at(0)
-    for slot in range(chain + 2 * reach):
-        fresh = None
-        token = own
+    token = own
+    finished = 0
+    for slot in range(chain + begin + reach):
         if slot < chain + reach:
             sums = own
             if slot - LAG in sent:
-                sums = (
-                    sums.astype(jnp.float32) + sent.pop(slot - LAG).astype(jnp.float32)
-                ).astype(jnp.bfloat16)
+                arrived = after(sent.pop(slot - LAG), token)
+                sums = (sums.astype(jnp.float32) + arrived.astype(jnp.float32)).astype(jnp.bfloat16)
             moving = [p for p in range(last) if 0 <= slot - LAG * p < chain]
             if moving:
                 sent[slot] = lax.ppermute(sums, axes, chain_pairs(stages, experts, moving)[0])
+            token = sums
             if slot >= reach:
-                fresh = activate(sums)
-            token = sums
+                fresh[slot + HOLD] = activate(sums)
+                token = fresh[slot + HOLD]
             if slot + 1 < chain + reach:
-                own = own_at(slot + 1, sums)
+                own = own_at(slot + 1, token)
                 token = own
-        if slot < reach:
+        if slot < begin:
             continue
-        arrived = told.pop(slot - LAG, None)
-        hidden = arrived if fresh is None else fresh
-        if fresh is not None and arrived is not None:
-            hidden = jnp.where(place == last, after(fresh, token), arrived)
-        moving = [p for p in range(last) if 0 <= slot - reach - LAG * (last - 1 - p) < chain]
+        hidden = fresh.get(slot)
+        if slot - LAG in told:
+            arrived = after(told.pop(slot - LAG), token)
+            hidden = arrived if hidden is None else jnp.where(place == last, hidden, arrived)
+        moving = [p for p in range(last) if 0 <= slot - begin - LAG * (last - 1 - p) < chain]
         if moving:
             told[slot] = lax.ppermute(hidden, axes, chain_pairs(stages, experts, moving)[1])
-        held = slot - reach - LAG * (last - place)
-        counts = ((held >= 0) & (held < chain)).astype(jnp.int32)
-        group.append((jnp.clip(held, 0, chain - 1), counts, hidden))
-        if len(group) == GROUP or slot == chain + 2 * reach - 1:
-            index = jnp.stack([jnp.stack([g[0] for g in group]), jnp.stack([g[1] for g in group])])
-            total = down_add(
-                index.astype(jnp.int32), jnp.stack([g[2] for g in group]), w_down, down_scale, total
-            )
-            group = []
-            if slot + 1 < chain + reach:
-                own = after(own, total)
-            elif slot - LAG + 1 in told:
-                told[slot - LAG + 1] = after(told[slot - LAG + 1], total)
+        held[slot] = hidden
+        token = hidden
+        complete = slot + 1 - begin - reach
+        if complete - finished >= GROUP or complete == chain:
+            units = list(range(finished, complete))
+            stacked = jnp.stack([hidden_of(u) for u in units])
+            index = jnp.array([units, [1] * len(units)], jnp.int32)
+            total = down_add(after(index, token), stacked, w_down, down_scale, total)
+            finished = complete
+            token = total
     return total if gathered is None else call_down(gathered, total)
 
 

time: 203 us -> 199 us (0.980)
  Pallas kernels: 89.8 us -> 76.1 us
  other arithmetic: 15.9 us -> 24.5 us
    pallas_call x14 -> x8, Pallas kernels: 39.7 us -> 26 us  [down_add(): pl.pallas_call(functools.partial(down_kernel, steps=steps), grid_spec=plt...]
    convert_element_type x12, other arithmetic: 9.06 us -> 14.6 us  [expert_rows(): (sums.astype(jnp.float32) + arrived.astype(jnp.float32)).astype(jnp.bfloa...]
    ppermute x12, waiting for transfers between devices: 27.8 us -> 23 us  [expert_rows(): lax.ppermute(hidden, axes, chain_pairs(stages, experts, moving)[1])]
    ppermute x12, waiting for transfers between devices: 0.6 us -> 2.84 us  [expert_rows(): lax.ppermute(sums, axes, chain_pairs(stages, experts, moving)[0])]
    select_n x6 -> x4, other arithmetic: 0.29 us -> 2.38 us  [expert_rows(): jnp.where(place == last, hidden, arrived)]
  transfers between devices with their start and end apart: 25 -> 25, of which waited for: 9 -> 10; matrix products, arithmetic and copies ran while one was open for 7% -> 12% of each run, Pallas kernels for 41% -> 35%
where the time goes in v3:
time: 199 us; the launch traced here: 197 us
  Pallas kernels  76.1 us (38%)
  starting transfers between devices  42.6 us (21%)
  waiting for transfers between devices  35.4 us (18%)
  other arithmetic  24.5 us (12%)
  blocking collectives  12.8 us (6%)
  local copies, waits for them, and re-layouts  2.83 us (1%)
  matrix products  2.26 us (1%)
    pallas_call x14, Pallas kernels, own_terms(): pl.pallas_call(own_kernel, grid_spec=pltpu.PrefetchScalarGridSpec(num_sca...  50.1 us
    pallas_call x8, Pallas kernels, down_add(): pl.pallas_call(functools.partial(down_kernel, steps=steps), grid_spec=plt...  26 us
    ppermute x12, starting transfers between devices, expert_rows(): lax.ppermute(sums, axes, chain_pairs(stages, experts, moving)[0])  24 us
    ppermute x12, waiting for transfers between devices, expert_rows(): lax.ppermute(hidden, axes, chain_pairs(stages, experts, moving)[1])  23 us
    convert_element_type x12, other arithmetic, expert_rows(): (sums.astype(jnp.float32) + arrived.astype(jnp.float32)).astype(jnp.bfloa...  14.6 us
    ppermute x12, starting transfers between devices, expert_rows(): lax.ppermute(hidden, axes, chain_pairs(stages, experts, moving)[1])  13.4 us
    all_to_all x1, blocking collectives, shards(): lax.all_to_all(partial_rows, 'expert', split_axis=0, concat_axis=0, tiled...  12.8 us
    all_to_all x1, waiting for transfers between devices, shards(): lax.all_to_all(outgoing, 'expert', split_axis=0, concat_axis=0, tiled=True)  9.56 us
  transfers between devices with their start and end apart: 25, of which 10 were waited for; matrix products, arithmetic and copies ran while one was open for 12% of the time, Pallas kernels for 35%

profile of v3, /device:TPU:0, one launch (start us, length us, event | category | flops | bytes accessed | tf_op | source)
XLA Modules:
  0.0 197.4 jit_solution(10513132371151878096)
XLA Ops:
  4.9 5.2 %all-to-all-start = ((bf16[8,24,1536]{2,1,0:T(8,128)(2,1)}), bf16[8,24,1536]{2,1,0:T(8,128)(2,1)S(1)}, u32[]{:S(2)}, u32[]{:S(2)}) async-start(bf16[8,24,1536]{2,1,0:T(8,128)(2,1)} %bitcast.28), calls=%async_computation | async-start | bytes 1179648 | tf_op jit(solution)/shard_map/all_to_all | solution.py:264
  10.9 9.6 %all-to-all-done = bf16[8,24,1536]{2,1,0:T(8,128)(2,1)S(1)} async-done(((bf16[8,24,1536]{2,1,0:T(8,128)(2,1)}), bf16[8,24,1536]{2,1,0:T(8,128)(2,1)S(1)}, u32[]{:S(2)}, u32[]{:S(2)}) %all-to-all-start) | async-done | bytes 589856 | tf_op jit(solution)/shard_map/all_to_all | solution.py:264
  20.5 4.3 %gate_up.14 = bf16[2,192,1024]{2,1,0:T(8,128)(2,1)S(1)} custom-call(s32[2]{0:T(128)S(1)} %pad_add_fusion.13.index_ref, bf16[192,1536]{1,0:T(8,128)(2,1)S(1)} %bitcast.170, bf16[1536,8192]{1,0:T(8,128)(2,1)} %gate_ref.27, bf16[1536,8192]{1,0:T(8,128)(2,1)} %up_ref.27, bf16[12,8192]{1,0:T(8,128)(2,1)S(1)} %bitcast.184, bf16[12,8192]{1,0:T(8,128)(2,1)S(1)} %bitcast.198), custom_call_target="tpu_custom_call" | custom-call | flops 37748736 | bytes 196608 | tf_op jit(solution)/shard_map/gate_up/pallas_call | solution.py:56
  26.8 4.3 %gate_up.15 = bf16[2,192,1024]{2,1,0:T(8,128)(2,1)S(1)} custom-call(s32[2]{0:T(128)S(1)} %pad_add_fusion.12.index_ref, bf16[192,1536]{1,0:T(8,128)(2,1)S(1)} %bitcast.171, bf16[1536,8192]{1,0:T(8,128)(2,1)} %gate_ref.27, bf16[1536,8192]{1,0:T(8,128)(2,1)} %up_ref.27, bf16[12,8192]{1,0:T(8,128)(2,1)S(1)} %bitcast.185, bf16[12,8192]{1,0:T(8,128)(2,1)S(1)} %bitcast.199), custom_call_target="tpu_custom_call" | custom-call | flops 37748736 | bytes 196608 | tf_op jit(solution)/shard_map/gate_up/pallas_call | solution.py:56
  33.4 4.3 %gate_up.16 = bf16[2,192,1024]{2,1,0:T(8,128)(2,1)S(1)} custom-call(s32[2]{0:T(128)S(1)} %pad_add_fusion.11.index_ref, bf16[192,1536]{1,0:T(8,128)(2,1)S(1)} %bitcast.172, bf16[1536,8192]{1,0:T(8,128)(2,1)} %gate_ref.27, bf16[1536,8192]{1,0:T(8,128)(2,1)} %up_ref.27, bf16[12,8192]{1,0:T(8,128)(2,1)S(1)} %bitcast.186, bf16[12,8192]{1,0:T(8,128)(2,1)S(1)} %bitcast.200), custom_call_target="tpu_custom_call" | custom-call | flops 37748736 | bytes 196608 | tf_op jit(solution)/shard_map/gate_up/pallas_call | solution.py:56
  38.9 3.7 %collective-permute-start.2 = (bf16[2,192,1024]{2,1,0:T(8,128)(2,1)}, bf16[2,192,1024]{2,1,0:T(8,128)(2,1)}, u32[]{:S(2)}, u32[]{:S(2)}) collective-permute-start(bf16[2,192,1024]{2,1,0:T(8,128)(2,1)} %add_convert_fusion.11), channel_id=1, source_target_pairs={{0,8},{8,16},{25,17},{17,9},{2,10},{10,18},{27,19},{19,11},{4,12},... | collective-permute-start | bytes 2359304 | tf_op jit(solution)/shard_map/ppermute | solution.py:214
  42.8 4.3 %gate_up.17 = bf16[2,192,1024]{2,1,0:T(8,128)(2,1)S(1)} custom-call(s32[2]{0:T(128)S(1)} %pad_add_fusion.10.index_ref, bf16[192,1536]{1,0:T(8,128)(2,1)S(1)} %bitcast.173, bf16[1536,8192]{1,0:T(8,128)(2,1)} %gate_ref.27, bf16[1536,8192]{1,0:T(8,128)(2,1)} %up_ref.27, bf16[12,8192]{1,0:T(8,128)(2,1)S(1)} %bitcast.187, bf16[12,8192]{1,0:T(8,128)(2,1)S(1)} %bitcast.201), custom_call_target="tpu_custom_call" | custom-call | flops 37748736 | bytes 196608 | tf_op jit(solution)/shard_map/gate_up/pallas_call | solution.py:56
  48.6 2.8 %collective-permute-start.3 = (bf16[2,192,1024]{2,1,0:T(8,128)(2,1)S(1)}, bf16[2,192,1024]{2,1,0:T(8,128)(2,1)}, u32[]{:S(2)}, u32[]{:S(2)}) collective-permute-start(bf16[2,192,1024]{2,1,0:T(8,128)(2,1)S(1)} %add_convert_fusion.10), channel_id=1, source_target_pairs={{0,8},{8,16},{25,17},{17,9},{2,10},{10,18},{27,19},{19,11},{4,12},... | collective-permute-start | bytes 2359304 | tf_op jit(solution)/shard_map/ppermute | solution.py:214
  51.5 4.3 %gate_up.18 = bf16[2,192,1024]{2,1,0:T(8,128)(2,1)S(1)} custom-call(s32[2]{0:T(128)S(1)} %pad_add_fusion.9.index_ref, bf16[192,1536]{1,0:T(8,128)(2,1)S(1)} %bitcast.174, bf16[1536,8192]{1,0:T(8,128)(2,1)} %gate_ref.27, bf16[1536,8192]{1,0:T(8,128)(2,1)} %up_ref.27, bf16[12,8192]{1,0:T(8,128)(2,1)S(1)} %bitcast.188, bf16[12,8192]{1,0:T(8,128)(2,1)S(1)} %bitcast.202), custom_call_target="tpu_custom_call" | custom-call | flops 37748736 | bytes 196608 | tf_op jit(solution)/shard_map/gate_up/pallas_call | solution.py:56
  60.1 4.3 %gate_up.19 = bf16[2,192,1024]{2,1,0:T(8,128)(2,1)S(1)} custom-call(s32[2]{0:T(128)S(1)} %pad_add_fusion.8.index_ref, bf16[192,1536]{1,0:T(8,128)(2,1)S(1)} %bitcast.175, bf16[1536,8192]{1,0:T(8,128)(2,1)} %gate_ref.27, bf16[1536,8192]{1,0:T(8,128)(2,1)} %up_ref.27, bf16[12,8192]{1,0:T(8,128)(2,1)S(1)} %bitcast.189, bf16[12,8192]{1,0:T(8,128)(2,1)S(1)} %bitcast.203), custom_call_target="tpu_custom_call" | custom-call | flops 37748736 | bytes 196608 | tf_op jit(solution)/shard_map/gate_up/pallas_call | solution.py:56
  68.4 4.3 %gate_up.20 = bf16[2,192,1024]{2,1,0:T(8,128)(2,1)S(1)} custom-call(s32[2]{0:T(128)S(1)} %pad_add_fusion.7.index_ref, bf16[192,1536]{1,0:T(8,128)(2,1)S(1)} %bitcast.176, bf16[1536,8192]{1,0:T(8,128)(2,1)} %gate_ref.27, bf16[1536,8192]{1,0:T(8,128)(2,1)} %up_ref.27, bf16[12,8192]{1,0:T(8,128)(2,1)S(1)} %bitcast.190, bf16[12,8192]{1,0:T(8,128)(2,1)S(1)} %bitcast.204), custom_call_target="tpu_custom_call" | custom-call | flops 37748736 | bytes 196608 | tf_op jit(solution)/shard_map/gate_up/pallas_call | solution.py:56
  77.8 4.3 %gate_up.21 = bf16[2,192,1024]{2,1,0:T(8,128)(2,1)S(1)} custom-call(s32[2]{0:T(128)S(1)} %pad_add_fusion.6.index_ref, bf16[192,1536]{1,0:T(8,128)(2,1)S(1)} %bitcast.177, bf16[1536,8192]{1,0:T(8,128)(2,1)} %gate_ref.27, bf16[1536,8192]{1,0:T(8,128)(2,1)} %up_ref.27, bf16[12,8192]{1,0:T(8,128)(2,1)S(1)} %bitcast.191, bf16[12,8192]{1,0:T(8,128)(2,1)S(1)} %bitcast.205), custom_call_target="tpu_custom_call" | custom-call | flops 37748736 | bytes 196608 | tf_op jit(solution)/shard_map/gate_up/pallas_call | solution.py:56
  123.9 11.1 %collective-permute-done.17 = bf16[192,1024]{1,0:T(8,128)(2,1)S(1)} collective-permute-done((bf16[192,1024]{1,0:T(8,128)(2,1)S(1)}, bf16[192,1024]{1,0:T(8,128)(2,1)S(1)}, u32[]{:S(2)}, u32[]{:S(2)}) %collective-permute-start.17) | collective-permute-done | bytes 393248 | tf_op jit(solution)/shard_map/ppermute | solution.py:230
  137.1 3.2 %down.8.total_ref = f32[192,1536]{1,0:T(8,128)S(1)} custom-call(s32[2,1]{1,0:T(2,128)S(1)} %copy-done.8, bf16[1,192,1024]{2,1,0:T(8,128)(2,1)S(1)} %get-tuple-element.99.hidden_ref, bf16[8192,1536]{1,0:T(8,128)(2,1)} %weight_ref.15, bf16[16,4,1536]{2,1,0:T(4,128)(2,1)S(1)} %convert_element_type.365.scale_ref, ...), custom_call_target="tpu_custom_call", output_to_operand_aliasing={{}: (4, {})} | custom-call | flops 18874368 | bytes 98304 | tf_op jit(solution)/shard_map/down/pallas_call | solution.py:110
  140.4 3.8 %collective-permute-done.16 = bf16[192,1024]{1,0:T(8,128)(2,1)S(1)} collective-permute-done((bf16[192,1024]{1,0:T(8,128)(2,1)S(1)}, bf16[192,1024]{1,0:T(8,128)(2,1)S(1)}, u32[]{:S(2)}, u32[]{:S(2)}) %collective-permute-start.16) | collective-permute-done | bytes 393248 | tf_op jit(solution)/shard_map/ppermute | solution.py:230
  146.2 3.2 %down.9.total_ref = f32[192,1536]{1,0:T(8,128)S(1)} custom-call(s32[2,1]{1,0:T(2,128)S(1)} %call_exported.0.index_ref, bf16[1,192,1024]{2,1,0:T(8,128)(2,1)S(1)} %get-tuple-element.97.hidden_ref, bf16[8192,1536]{1,0:T(8,128)(2,1)} %weight_ref.15, bf16[16,4,1536]{2,1,0:T(4,128)(2,1)S(1)} %convert_element_type.365.scale_ref, ...), custom_call_target="tpu_custom_call", output_to_operand_aliasing={{}: (4, {})} | custom-call | flops 18874368 | bytes 98304 | tf_op jit(solution)/shard_map/down/pallas_call | solution.py:110
  151.2 3.2 %down.10.total_ref = f32[192,1536]{1,0:T(8,128)S(1)} custom-call(s32[2,1]{1,0:T(2,128)S(1)} %copy-done.7, bf16[1,192,1024]{2,1,0:T(8,128)(2,1)S(1)} %select_bitcast_fusion.5.hidden_ref, bf16[8192,1536]{1,0:T(8,128)(2,1)} %weight_ref.15, bf16[16,4,1536]{2,1,0:T(4,128)(2,1)S(1)} %convert_element_type.365.scale_ref, ...), custom_call_target="tpu_custom_call", output_to_operand_aliasing={{}: (4, {})} | custom-call | flops 18874368 | bytes 98304 | tf_op jit(solution)/shard_map/down/pallas_call | solution.py:110
  154.4 5.5 %collective-permute-done.18 = bf16[192,1024]{1,0:T(8,128)(2,1)S(1)} collective-permute-done((bf16[192,1024]{1,0:T(8,128)(2,1)S(1)}, bf16[192,1024]{1,0:T(8,128)(2,1)S(1)}, u32[]{:S(2)}, u32[]{:S(2)}) %collective-permute-start.18) | collective-permute-done | bytes 393248 | tf_op jit(solution)/shard_map/ppermute | solution.py:230
  161.5 3.2 %down.11.total_ref = f32[192,1536]{1,0:T(8,128)S(1)} custom-call(s32[2,1]{1,0:T(2,128)S(1)} %copy-done.6, bf16[1,192,1024]{2,1,0:T(8,128)(2,1)S(1)} %select_bitcast_fusion.4.hidden_ref, bf16[8192,1536]{1,0:T(8,128)(2,1)} %weight_ref.15, bf16[16,4,1536]{2,1,0:T(4,128)(2,1)S(1)} %convert_element_type.365.scale_ref, ...), custom_call_target="tpu_custom_call", output_to_operand_aliasing={{}: (4, {})} | custom-call | flops 18874368 | bytes 98304 | tf_op jit(solution)/shard_map/down/pallas_call | solution.py:110
  166.5 3.2 %down.12.total_ref = f32[192,1536]{1,0:T(8,128)S(1)} custom-call(s32[2,1]{1,0:T(2,128)S(1)} %copy-done.5, bf16[1,192,1024]{2,1,0:T(8,128)(2,1)S(1)} %select_bitcast_fusion.3.hidden_ref, bf16[8192,1536]{1,0:T(8,128)(2,1)} %weight_ref.15, bf16[16,4,1536]{2,1,0:T(4,128)(2,1)S(1)} %convert_element_type.365.scale_ref, ...), custom_call_target="tpu_custom_call", output_to_operand_aliasing={{}: (4, {})} | custom-call | flops 18874368 | bytes 98304 | tf_op jit(solution)/shard_map/down/pallas_call | solution.py:110
  171.8 3.2 %down.13.total_ref = f32[192,1536]{1,0:T(8,128)S(1)} custom-call(s32[2,1]{1,0:T(2,128)S(1)} %copy-done.4, bf16[1,192,1024]{2,1,0:T(8,128)(2,1)S(1)} %select_bitcast_fusion.2.hidden_ref, bf16[8192,1536]{1,0:T(8,128)(2,1)} %weight_ref.15, bf16[16,4,1536]{2,1,0:T(4,128)(2,1)S(1)} %convert_element_type.365.scale_ref, ...), custom_call_target="tpu_custom_call", output_to_operand_aliasing={{}: (4, {})} | custom-call | flops 18874368 | bytes 98304 | tf_op jit(solution)/shard_map/down/pallas_call | solution.py:110
  175.7 3.2 %down.14.total_ref = f32[192,1536]{1,0:T(8,128)S(1)} custom-call(s32[2,1]{1,0:T(2,128)S(1)} %copy-done.3, bf16[1,192,1024]{2,1,0:T(8,128)(2,1)S(1)} %select_bitcast_fusion.1.hidden_ref, bf16[8192,1536]{1,0:T(8,128)(2,1)} %weight_ref.15, bf16[16,4,1536]{2,1,0:T(4,128)(2,1)S(1)} %convert_element_type.365.scale_ref, ...), custom_call_target="tpu_custom_call", output_to_operand_aliasing={{}: (4, {})} | custom-call | flops 18874368 | bytes 98304 | tf_op jit(solution)/shard_map/down/pallas_call | solution.py:110
  180.2 3.2 %down.15 = f32[192,1536]{1,0:T(8,128)S(1)} custom-call(s32[2,1]{1,0:T(2,128)S(1)} %copy-done.2, bf16[1,192,1024]{2,1,0:T(8,128)(2,1)S(1)} %select_bitcast_fusion.hidden_ref, bf16[8192,1536]{1,0:T(8,128)(2,1)} %weight_ref.15, bf16[16,4,1536]{2,1,0:T(4,128)(2,1)S(1)} %convert_element_type.365.scale_ref, ...), custom_call_target="tpu_custom_call", output_to_operand_aliasing={{}: (4, {})} | custom-call | flops 18874368 | bytes 98304 | tf_op jit(solution)/shard_map/down/pallas_call | solution.py:110
  183.5 12.8 %all_to_all.23 = bf16[8,24,1536]{2,1,0:T(8,128)(2,1)S(1)} all-to-all(bf16[8,24,1536]{2,1,0:T(8,128)(2,1)S(1)} %bitcast.212), channel_id=1, replica_groups=mesh['fsdp'=4,'expert'=8] {'expert'}, dimensions={0} | all-to-all | bytes 1179648 | tf_op jit(solution)/shard_map/all_to_all | solution.py:267
  (141 shorter events, 81.6 us)
Async XLA Ops:
  4.9 15.6 %all-to-all-start = ((bf16[8,24,1536]{2,1,0:T(8,128)(2,1)}), bf16[8,24,1536]{2,1,0:T(8,128)(2,1)S(1)}, u32[]{:S(2)}, u32[]{:S(2)}) async-start(bf16[8,24,1536]{2,1,0:T(8,128)(2,1)} %bitcast.28), calls=%async_computation | async-start | bytes 1179648 | tf_op jit(solution)/shard_map/all_to_all | solution.py:264
  24.8 12.8 %collective-permute-start = (bf16[2,192,1024]{2,1,0:T(8,128)(2,1)S(1)}, bf16[2,192,1024]{2,1,0:T(8,128)(2,1)S(1)}, u32[]{:S(2)}, u32[]{:S(2)}) collective-permute-start(bf16[2,192,1024]{2,1,0:T(8,128)(2,1)S(1)} %gate_up.14), channel_id=1, source_target_pairs={{0,8},{25,17},{2,10},{27,19},{4,12},{29,21},{6,14},{31,23}} | collective-permute-start | bytes 2359304 | tf_op jit(solution)/shard_map/ppermute | solution.py:214
  31.1 16.0 %collective-permute-start.1 = (bf16[2,192,1024]{2,1,0:T(8,128)(2,1)S(1)}, bf16[2,192,1024]{2,1,0:T(8,128)(2,1)}, u32[]{:S(2)}, u32[]{:S(2)}) collective-permute-start(bf16[2,192,1024]{2,1,0:T(8,128)(2,1)S(1)} %gate_up.15), channel_id=1, source_target_pairs={{0,8},{25,17},{2,10},{27,19},{4,12},{29,21},{6,14},{31,23}} | collective-permute-start | bytes 2359304 | tf_op jit(solution)/shard_map/ppermute | solution.py:214
  38.9 16.9 %collective-permute-start.2 = (bf16[2,192,1024]{2,1,0:T(8,128)(2,1)}, bf16[2,192,1024]{2,1,0:T(8,128)(2,1)}, u32[]{:S(2)}, u32[]{:S(2)}) collective-permute-start(bf16[2,192,1024]{2,1,0:T(8,128)(2,1)} %add_convert_fusion.11), channel_id=1, source_target_pairs={{0,8},{8,16},{25,17},{17,9},{2,10},{10,18},{27,19},{19,11},{4,12},... | collective-permute-start | bytes 2359304 | tf_op jit(solution)/shard_map/ppermute | solution.py:214
  48.6 15.8 %collective-permute-start.3 = (bf16[2,192,1024]{2,1,0:T(8,128)(2,1)S(1)}, bf16[2,192,1024]{2,1,0:T(8,128)(2,1)}, u32[]{:S(2)}, u32[]{:S(2)}) collective-permute-start(bf16[2,192,1024]{2,1,0:T(8,128)(2,1)S(1)} %add_convert_fusion.10), channel_id=1, source_target_pairs={{0,8},{8,16},{25,17},{17,9},{2,10},{10,18},{27,19},{19,11},{4,12},... | collective-permute-start | bytes 2359304 | tf_op jit(solution)/shard_map/ppermute | solution.py:214
  57.3 15.4 %collective-permute-start.4 = (bf16[2,192,1024]{2,1,0:T(8,128)(2,1)S(1)}, bf16[2,192,1024]{2,1,0:T(8,128)(2,1)}, u32[]{:S(2)}, u32[]{:S(2)}) collective-permute-start(bf16[2,192,1024]{2,1,0:T(8,128)(2,1)S(1)} %add_convert_fusion.9), channel_id=1, source_target_pairs={{0,8},{8,16},{16,24},{25,17},{17,9},{9,1},{2,10},{10,18},{18,26},{... | collective-permute-start | bytes 2359304 | tf_op jit(solution)/shard_map/ppermute | solution.py:214
  65.8 16.3 %collective-permute-start.5 = (bf16[2,192,1024]{2,1,0:T(8,128)(2,1)S(1)}, bf16[2,192,1024]{2,1,0:T(8,128)(2,1)}, u32[]{:S(2)}, u32[]{:S(2)}) collective-permute-start(bf16[2,192,1024]{2,1,0:T(8,128)(2,1)S(1)} %add_convert_fusion.8), channel_id=1, source_target_pairs={{0,8},{8,16},{16,24},{25,17},{17,9},{9,1},{2,10},{10,18},{18,26},{... | collective-permute-start | bytes 2359304 | tf_op jit(solution)/shard_map/ppermute | solution.py:214
  74.2 15.3 %collective-permute-start.6 = (bf16[2,192,1024]{2,1,0:T(8,128)(2,1)S(1)}, bf16[2,192,1024]{2,1,0:T(8,128)(2,1)}, u32[]{:S(2)}, u32[]{:S(2)}) collective-permute-start(bf16[2,192,1024]{2,1,0:T(8,128)(2,1)S(1)} %add_convert_fusion.7), channel_id=1, source_target_pairs={{0,8},{8,16},{16,24},{25,17},{17,9},{9,1},{2,10},{10,18},{18,26},{... | collective-permute-start | bytes 2359304 | tf_op jit(solution)/shard_map/ppermute | solution.py:214
  83.6 14.7 %collective-permute-start.7 = (bf16[2,192,1024]{2,1,0:T(8,128)(2,1)S(1)}, bf16[2,192,1024]{2,1,0:T(8,128)(2,1)}, u32[]{:S(2)}, u32[]{:S(2)}) collective-permute-start(bf16[2,192,1024]{2,1,0:T(8,128)(2,1)S(1)} %add_convert_fusion.6), channel_id=1, source_target_pairs={{0,8},{8,16},{16,24},{25,17},{17,9},{9,1},{2,10},{10,18},{18,26},{... | collective-permute-start | bytes 2359304 | tf_op jit(solution)/shard_map/ppermute | solution.py:214
  91.8 13.9 %collective-permute-start.8 = (bf16[2,192,1024]{2,1,0:T(8,128)(2,1)}, bf16[2,192,1024]{2,1,0:T(8,128)(2,1)}, u32[]{:S(2)}, u32[]{:S(2)}) collective-permute-start(bf16[2,192,1024]{2,1,0:T(8,128)(2,1)} %add_convert_fusion.5), channel_id=1, source_target_pairs={{8,16},{16,24},{17,9},{9,1},{10,18},{18,26},{19,11},{11,3},{12,20}... | collective-permute-start | bytes 2359304 | tf_op jit(solution)/shard_map/ppermute | solution.py:214
  93.9 16.6 %collective-permute-start.10 = (bf16[192,1024]{1,0:T(8,128)(2,1)}, bf16[192,1024]{1,0:T(8,128)(2,1)S(1)}, u32[]{:S(2)}, u32[]{:S(2)}) collective-permute-start(bf16[192,1024]{1,0:T(8,128)(2,1)} %fusion.39), channel_id=1, source_target_pairs={{24,16},{1,9},{26,18},{3,11},{28,20},{5,13},{30,22},{7,15}} | collective-permute-start | bytes 1179656 | tf_op jit(solution)/shard_map/ppermute | solution.py:230
  94.8 21.5 %collective-permute-start.12 = (bf16[192,1024]{1,0:T(8,128)(2,1)}, bf16[192,1024]{1,0:T(8,128)(2,1)S(1)}, u32[]{:S(2)}, u32[]{:S(2)}) collective-permute-start(bf16[192,1024]{1,0:T(8,128)(2,1)} %fusion.38), channel_id=1, source_target_pairs={{24,16},{1,9},{26,18},{3,11},{28,20},{5,13},{30,22},{7,15}} | collective-permute-start | bytes 1179656 | tf_op jit(solution)/shard_map/ppermute | solution.py:230
  102.3 10.3 %collective-permute-start.9 = (bf16[2,192,1024]{2,1,0:T(8,128)(2,1)S(1)}, bf16[2,192,1024]{2,1,0:T(8,128)(2,1)S(1)}, u32[]{:S(2)}, u32[]{:S(2)}) collective-permute-start(bf16[2,192,1024]{2,1,0:T(8,128)(2,1)S(1)} %add_convert_fusion.4), channel_id=1, source_target_pairs={{8,16},{16,24},{17,9},{9,1},{10,18},{18,26},{19,11},{11,3},{12,20}... | collective-permute-start | bytes 2359304 | tf_op jit(solution)/shard_map/ppermute | solution.py:214
  107.1 10.2 %collective-permute-start.11 = (bf16[2,192,1024]{2,1,0:T(8,128)(2,1)S(1)}, bf16[2,192,1024]{2,1,0:T(8,128)(2,1)S(1)}, u32[]{:S(2)}, u32[]{:S(2)}) collective-permute-start(bf16[2,192,1024]{2,1,0:T(8,128)(2,1)S(1)} %add_convert_fusion.3), channel_id=1, source_target_pairs={{16,24},{9,1},{18,26},{11,3},{20,28},{13,5},{22,30},{15,7}} | collective-permute-start | bytes 2359304 | tf_op jit(solution)/shard_map/ppermute | solution.py:214
  111.9 8.3 %collective-permute-start.14 = (bf16[192,1024]{1,0:T(8,128)(2,1)S(1)}, bf16[192,1024]{1,0:T(8,128)(2,1)S(1)}, u32[]{:S(2)}, u32[]{:S(2)}) collective-permute-start(bf16[192,1024]{1,0:T(8,128)(2,1)S(1)} %broadcast_select_fusion.5), channel_id=1, source_target_pairs={{16,8},{24,16},{9,17},{1,9},{18,10},{26,18},{11,19},{3,11},{20,12}... | collective-permute-start | bytes 1179656 | tf_op jit(solution)/shard_map/ppermute | solution.py:230
  112.9 8.9 %collective-permute-start.13 = (bf16[2,192,1024]{2,1,0:T(8,128)(2,1)S(1)}, bf16[2,192,1024]{2,1,0:T(8,128)(2,1)S(1)}, u32[]{:S(2)}, u32[]{:S(2)}) collective-permute-start(bf16[2,192,1024]{2,1,0:T(8,128)(2,1)S(1)} %add_convert_fusion.2), channel_id=1, source_target_pairs={{16,24},{9,1},{18,26},{11,3},{20,28},{13,5},{22,30},{15,7}} | collective-permute-start | bytes 2359304 | tf_op jit(solution)/shard_map/ppermute | solution.py:214
  120.6 14.4 %collective-permute-start.17 = (bf16[192,1024]{1,0:T(8,128)(2,1)S(1)}, bf16[192,1024]{1,0:T(8,128)(2,1)S(1)}, u32[]{:S(2)}, u32[]{:S(2)}) collective-permute-start(bf16[192,1024]{1,0:T(8,128)(2,1)S(1)} %broadcast_select_fusion.3), channel_id=1, source_target_pairs={{8,0},{16,8},{24,16},{17,25},{9,17},{1,9},{10,2},{18,10},{26,18},{... | collective-permute-start | bytes 1179656 | tf_op jit(solution)/shard_map/ppermute | solution.py:230
  122.6 21.6 %collective-permute-start.16 = (bf16[192,1024]{1,0:T(8,128)(2,1)S(1)}, bf16[192,1024]{1,0:T(8,128)(2,1)S(1)}, u32[]{:S(2)}, u32[]{:S(2)}) collective-permute-start(bf16[192,1024]{1,0:T(8,128)(2,1)S(1)} %broadcast_select_fusion.2), channel_id=1, source_target_pairs={{8,0},{16,8},{24,16},{17,25},{9,17},{1,9},{10,2},{18,10},{26,18},{... | collective-permute-start | bytes 1179656 | tf_op jit(solution)/shard_map/ppermute | solution.py:230
  135.7 14.1 %collective-permute-start.19 = (bf16[192,1024]{1,0:T(8,128)(2,1)S(1)}, bf16[192,1024]{1,0:T(8,128)(2,1)S(1)}, u32[]{:S(2)}, u32[]{:S(2)}) collective-permute-start(bf16[192,1024]{1,0:T(8,128)(2,1)S(1)} %get-tuple-element.100), channel_id=1, source_target_pairs={{8,0},{16,8},{24,16},{17,25},{9,17},{1,9},{10,2},{18,10},{26,18},{... | collective-permute-start | bytes 1179656 | tf_op jit(solution)/shard_map/ppermute | solution.py:230
  144.9 15.0 %collective-permute-start.18 = (bf16[192,1024]{1,0:T(8,128)(2,1)S(1)}, bf16[192,1024]{1,0:T(8,128)(2,1)S(1)}, u32[]{:S(2)}, u32[]{:S(2)}) collective-permute-start(bf16[192,1024]{1,0:T(8,128)(2,1)S(1)} %get-tuple-element.98), channel_id=1, source_target_pairs={{8,0},{16,8},{24,16},{17,25},{9,17},{1,9},{10,2},{18,10},{26,18},{... | collective-permute-start | bytes 1179656 | tf_op jit(solution)/shard_map/ppermute | solution.py:230
  149.8 15.3 %collective-permute-start.21 = (bf16[192,1024]{1,0:T(8,128)(2,1)S(1)}, bf16[192,1024]{1,0:T(8,128)(2,1)S(1)}, u32[]{:S(2)}, u32[]{:S(2)}) collective-permute-start(bf16[192,1024]{1,0:T(8,128)(2,1)S(1)} %collective-permute-done.19), channel_id=1, source_target_pairs={{8,0},{16,8},{17,25},{9,17},{10,2},{18,10},{19,27},{11,19},{12,4},... | collective-permute-start | bytes 1179656 | tf_op jit(solution)/shard_map/ppermute | solution.py:230
  159.9 10.5 %collective-permute-start.20 = (bf16[192,1024]{1,0:T(8,128)(2,1)S(1)}, bf16[192,1024]{1,0:T(8,128)(2,1)S(1)}, u32[]{:S(2)}, u32[]{:S(2)}) collective-permute-start(bf16[192,1024]{1,0:T(8,128)(2,1)S(1)} %collective-permute-done.18), channel_id=1, source_target_pairs={{8,0},{16,8},{17,25},{9,17},{10,2},{18,10},{19,27},{11,19},{12,4},... | collective-permute-start | bytes 1179656 | tf_op jit(solution)/shard_map/ppermute | solution.py:230
  165.1 10.2 %collective-permute-start.23 = (bf16[192,1024]{1,0:T(8,128)(2,1)S(1)}, bf16[192,1024]{1,0:T(8,128)(2,1)S(1)}, u32[]{:S(2)}, u32[]{:S(2)}) collective-permute-start(bf16[192,1024]{1,0:T(8,128)(2,1)S(1)} %collective-permute-done.21), channel_id=1, source_target_pairs={{8,0},{17,25},{10,2},{19,27},{12,4},{21,29},{14,6},{23,31}} | collective-permute-start | bytes 1179656 | tf_op jit(solution)/shard_map/ppermute | solution.py:230
  170.4 9.7 %collective-permute-start.22 = (bf16[192,1024]{1,0:T(8,128)(2,1)S(1)}, bf16[192,1024]{1,0:T(8,128)(2,1)S(1)}, u32[]{:S(2)}, u32[]{:S(2)}) collective-permute-start(bf16[192,1024]{1,0:T(8,128)(2,1)S(1)} %collective-permute-done.20), channel_id=1, source_target_pairs={{8,0},{17,25},{10,2},{19,27},{12,4},{21,29},{14,6},{23,31}} | collective-permute-start | bytes 1179656 | tf_op jit(solution)/shard_map/ppermute | solution.py:230
  (14 other events, 89.3 us)

commit v4 on v3

--- a/solution.py
+++ b/solution.py
@@ -216,10 +216,9 @@
             if slot >= reach:
                 fresh[slot + HOLD] = activate(sums)
                 token = fresh[slot + HOLD]
-            if slot + 1 < chain + reach:
-                own = own_at(slot + 1, token)
-                token = own
         if slot < begin:
+            own = own_at(slot + 1, token)
+            token = own
             continue
         hidden = fresh.get(slot)
         if slot - LAG in told:
@@ -230,6 +229,9 @@
             told[slot] = lax.ppermute(hidden, axes, chain_pairs(stages, experts, moving)[1])
         held[slot] = hidden
         token = hidden
+        if slot + 1 < chain + reach:
+            own = own_at(slot + 1, token)
+            token = own
         complete = slot + 1 - begin - reach
         if complete - finished >= GROUP or complete == chain:
             units = list(range(finished, complete))

time: 199 us -> 198 us (level)
  other arithmetic: 24.5 us -> 22.4 us
    ppermute x12, waiting for transfers between devices: 23 us -> 25.4 us  [expert_rows(): lax.ppermute(hidden, axes, chain_pairs(stages, experts, moving)[1])]
    ppermute x12, waiting for transfers between devices: 2.84 us -> 0.67 us  [expert_rows(): lax.ppermute(sums, axes, chain_pairs(stages, experts, moving)[0])]
  transfers between devices with their start and end apart: 25 -> 25, of which waited for: 10 -> 10; matrix products, arithmetic and copies ran while one was open for 12% -> 11% of each run, Pallas kernels for 35% -> 35%
where the time goes in v4:
time: 198 us; the launch traced here: 196 us
  Pallas kernels  76.1 us (38%)
  starting transfers between devices  43.5 us (22%)
  waiting for transfers between devices  35.6 us (18%)
  other arithmetic  22.4 us (11%)
  blocking collectives  12.8 us (6%)
  local copies, waits for them, and re-layouts  2.83 us (1%)
  matrix products  2.26 us (1%)
    pallas_call x14, Pallas kernels, own_terms(): pl.pallas_call(own_kernel, grid_spec=pltpu.PrefetchScalarGridSpec(num_sca...  50.2 us
    pallas_call x8, Pallas kernels, down_add(): pl.pallas_call(functools.partial(down_kernel, steps=steps), grid_spec=plt...  26 us
    ppermute x12, waiting for transfers between devices, expert_rows(): lax.ppermute(hidden, axes, chain_pairs(stages, experts, moving)[1])  25.4 us
    ppermute x12, starting transfers between devices, expert_rows(): lax.ppermute(sums, axes, chain_pairs(stages, experts, moving)[0])  25.1 us
    ppermute x12, starting transfers between devices, expert_rows(): lax.ppermute(hidden, axes, chain_pairs(stages, experts, moving)[1])  13.2 us
    convert_element_type x12, other arithmetic, expert_rows(): (sums.astype(jnp.float32) + arrived.astype(jnp.float32)).astype(jnp.bfloa...  13.2 us
    all_to_all x1, blocking collectives, shards(): lax.all_to_all(partial_rows, 'expert', split_axis=0, concat_axis=0, tiled...  12.8 us
    all_to_all x1, waiting for transfers between devices, shards(): lax.all_to_all(outgoing, 'expert', split_axis=0, concat_axis=0, tiled=True)  9.56 us
  transfers between devices with their start and end apart: 25, of which 10 were waited for; matrix products, arithmetic and copies ran while one was open for 11% of the time, Pallas kernels for 35%

profile of v4, /device:TPU:0, one launch (start us, length us, event | category | flops | bytes accessed | tf_op | source)
XLA Modules:
  0.0 196.4 jit_solution(4168620574476474232)
XLA Ops:
  4.9 5.2 %all-to-all-start = ((bf16[8,24,1536]{2,1,0:T(8,128)(2,1)}), bf16[8,24,1536]{2,1,0:T(8,128)(2,1)S(1)}, u32[]{:S(2)}, u32[]{:S(2)}) async-start(bf16[8,24,1536]{2,1,0:T(8,128)(2,1)} %bitcast.20), calls=%async_computation | async-start | bytes 1179648 | tf_op jit(solution)/shard_map/all_to_all | solution.py:266
  10.9 9.6 %all-to-all-done = bf16[8,24,1536]{2,1,0:T(8,128)(2,1)S(1)} async-done(((bf16[8,24,1536]{2,1,0:T(8,128)(2,1)}), bf16[8,24,1536]{2,1,0:T(8,128)(2,1)S(1)}, u32[]{:S(2)}, u32[]{:S(2)}) %all-to-all-start) | async-done | bytes 589856 | tf_op jit(solution)/shard_map/all_to_all | solution.py:266
  20.5 4.3 %gate_up.14 = bf16[2,192,1024]{2,1,0:T(8,128)(2,1)S(1)} custom-call(s32[2]{0:T(128)S(1)} %pad_add_fusion.9.index_ref, bf16[192,1536]{1,0:T(8,128)(2,1)S(1)} %bitcast.162, bf16[1536,8192]{1,0:T(8,128)(2,1)} %gate_ref.27, bf16[1536,8192]{1,0:T(8,128)(2,1)} %up_ref.27, bf16[12,8192]{1,0:T(8,128)(2,1)S(1)} %bitcast.176, bf16[12,8192]{1,0:T(8,128)(2,1)S(1)} %bitcast.190), custom_call_target="tpu_custom_call" | custom-call | flops 37748736 | bytes 196608 | tf_op jit(solution)/shard_map/gate_up/pallas_call | solution.py:56
  26.8 4.3 %gate_up.15 = bf16[2,192,1024]{2,1,0:T(8,128)(2,1)S(1)} custom-call(s32[2]{0:T(128)S(1)} %pad_add_fusion.8.index_ref, bf16[192,1536]{1,0:T(8,128)(2,1)S(1)} %bitcast.163, bf16[1536,8192]{1,0:T(8,128)(2,1)} %gate_ref.27, bf16[1536,8192]{1,0:T(8,128)(2,1)} %up_ref.27, bf16[12,8192]{1,0:T(8,128)(2,1)S(1)} %bitcast.177, bf16[12,8192]{1,0:T(8,128)(2,1)S(1)} %bitcast.191), custom_call_target="tpu_custom_call" | custom-call | flops 37748736 | bytes 196608 | tf_op jit(solution)/shard_map/gate_up/pallas_call | solution.py:56
  33.4 4.3 %gate_up.16 = bf16[2,192,1024]{2,1,0:T(8,128)(2,1)S(1)} custom-call(s32[2]{0:T(128)S(1)} %pad_add_fusion.7.index_ref, bf16[192,1536]{1,0:T(8,128)(2,1)S(1)} %bitcast.164, bf16[1536,8192]{1,0:T(8,128)(2,1)} %gate_ref.27, bf16[1536,8192]{1,0:T(8,128)(2,1)} %up_ref.27, bf16[12,8192]{1,0:T(8,128)(2,1)S(1)} %bitcast.178, bf16[12,8192]{1,0:T(8,128)(2,1)S(1)} %bitcast.192), custom_call_target="tpu_custom_call" | custom-call | flops 37748736 | bytes 196608 | tf_op jit(solution)/shard_map/gate_up/pallas_call | solution.py:56
  38.0 2.8 %collective-permute-start.2 = (bf16[2,192,1024]{2,1,0:T(8,128)(2,1)S(1)}, bf16[2,192,1024]{2,1,0:T(8,128)(2,1)S(1)}, u32[]{:S(2)}, u32[]{:S(2)}) collective-permute-start(bf16[2,192,1024]{2,1,0:T(8,128)(2,1)S(1)} %add_convert_fusion.11), channel_id=1, source_target_pairs={{0,8},{8,16},{25,17},{17,9},{2,10},{10,18},{27,19},{19,11},{4,12},... | collective-permute-start | bytes 2359304 | tf_op jit(solution)/shard_map/ppermute | solution.py:214
  41.0 4.3 %gate_up.17 = bf16[2,192,1024]{2,1,0:T(8,128)(2,1)S(1)} custom-call(s32[2]{0:T(128)S(1)} %pad_add_fusion.6.index_ref, bf16[192,1536]{1,0:T(8,128)(2,1)S(1)} %bitcast.165, bf16[1536,8192]{1,0:T(8,128)(2,1)} %gate_ref.27, bf16[1536,8192]{1,0:T(8,128)(2,1)} %up_ref.27, bf16[12,8192]{1,0:T(8,128)(2,1)S(1)} %bitcast.179, bf16[12,8192]{1,0:T(8,128)(2,1)S(1)} %bitcast.193), custom_call_target="tpu_custom_call" | custom-call | flops 37748736 | bytes 196608 | tf_op jit(solution)/shard_map/gate_up/pallas_call | solution.py:56
  47.6 4.7 %collective-permute-start.3 = (bf16[2,192,1024]{2,1,0:T(8,128)(2,1)}, bf16[2,192,1024]{2,1,0:T(8,128)(2,1)}, u32[]{:S(2)}, u32[]{:S(2)}) collective-permute-start(bf16[2,192,1024]{2,1,0:T(8,128)(2,1)} %add_convert_fusion.10), channel_id=1, source_target_pairs={{0,8},{8,16},{25,17},{17,9},{2,10},{10,18},{27,19},{19,11},{4,12},... | collective-permute-start | bytes 2359304 | tf_op jit(solution)/shard_map/ppermute | solution.py:214
  52.4 4.3 %gate_up.18 = bf16[2,192,1024]{2,1,0:T(8,128)(2,1)S(1)} custom-call(s32[2]{0:T(128)S(1)} %pad_add_fusion.5.index_ref, bf16[192,1536]{1,0:T(8,128)(2,1)S(1)} %bitcast.166, bf16[1536,8192]{1,0:T(8,128)(2,1)} %gate_ref.27, bf16[1536,8192]{1,0:T(8,128)(2,1)} %up_ref.27, bf16[12,8192]{1,0:T(8,128)(2,1)S(1)} %bitcast.180, bf16[12,8192]{1,0:T(8,128)(2,1)S(1)} %bitcast.194), custom_call_target="tpu_custom_call" | custom-call | flops 37748736 | bytes 196608 | tf_op jit(solution)/shard_map/gate_up/pallas_call | solution.py:56
  58.5 4.3 %gate_up.19 = bf16[2,192,1024]{2,1,0:T(8,128)(2,1)S(1)} custom-call(s32[2]{0:T(128)S(1)} %pad_add_fusion.4.index_ref, bf16[192,1536]{1,0:T(8,128)(2,1)S(1)} %bitcast.167, bf16[1536,8192]{1,0:T(8,128)(2,1)} %gate_ref.27, bf16[1536,8192]{1,0:T(8,128)(2,1)} %up_ref.27, bf16[12,8192]{1,0:T(8,128)(2,1)S(1)} %bitcast.181, bf16[12,8192]{1,0:T(8,128)(2,1)S(1)} %bitcast.195), custom_call_target="tpu_custom_call" | custom-call | flops 37748736 | bytes 196608 | tf_op jit(solution)/shard_map/gate_up/pallas_call | solution.py:56
  65.1 4.0 %collective-permute-start.5 = (bf16[2,192,1024]{2,1,0:T(8,128)(2,1)}, bf16[2,192,1024]{2,1,0:T(8,128)(2,1)}, u32[]{:S(2)}, u32[]{:S(2)}) collective-permute-start(bf16[2,192,1024]{2,1,0:T(8,128)(2,1)} %add_convert_fusion.8), channel_id=1, source_target_pairs={{0,8},{8,16},{16,24},{25,17},{17,9},{9,1},{2,10},{10,18},{18,26},{... | collective-permute-start | bytes 2359304 | tf_op jit(solution)/shard_map/ppermute | solution.py:214
  69.3 4.3 %gate_up.20 = bf16[2,192,1024]{2,1,0:T(8,128)(2,1)S(1)} custom-call(s32[2]{0:T(128)S(1)} %pad_add_fusion.3.index_ref, bf16[192,1536]{1,0:T(8,128)(2,1)S(1)} %bitcast.168, bf16[1536,8192]{1,0:T(8,128)(2,1)} %gate_ref.27, bf16[1536,8192]{1,0:T(8,128)(2,1)} %up_ref.27, bf16[12,8192]{1,0:T(8,128)(2,1)S(1)} %bitcast.182, bf16[12,8192]{1,0:T(8,128)(2,1)S(1)} %bitcast.196), custom_call_target="tpu_custom_call" | custom-call | flops 37748736 | bytes 196608 | tf_op jit(solution)/shard_map/gate_up/pallas_call | solution.py:56
  77.3 4.3 %gate_up.21 = bf16[2,192,1024]{2,1,0:T(8,128)(2,1)S(1)} custom-call(s32[2]{0:T(128)S(1)} %pad_add_fusion.2.index_ref, bf16[192,1536]{1,0:T(8,128)(2,1)S(1)} %bitcast.169, bf16[1536,8192]{1,0:T(8,128)(2,1)} %gate_ref.27, bf16[1536,8192]{1,0:T(8,128)(2,1)} %up_ref.27, bf16[12,8192]{1,0:T(8,128)(2,1)S(1)} %bitcast.183, bf16[12,8192]{1,0:T(8,128)(2,1)S(1)} %bitcast.197), custom_call_target="tpu_custom_call" | custom-call | flops 37748736 | bytes 196608 | tf_op jit(solution)/shard_map/gate_up/pallas_call | solution.py:56
  120.5 14.3 %collective-permute-done.17 = bf16[192,1024]{1,0:T(8,128)(2,1)S(1)} collective-permute-done((bf16[192,1024]{1,0:T(8,128)(2,1)S(1)}, bf16[192,1024]{1,0:T(8,128)(2,1)S(1)}, u32[]{:S(2)}, u32[]{:S(2)}) %collective-permute-start.17) | collective-permute-done | bytes 393248 | tf_op jit(solution)/shard_map/ppermute | solution.py:229
  136.9 3.2 %down.8.total_ref = f32[192,1536]{1,0:T(8,128)S(1)} custom-call(s32[2,1]{1,0:T(2,128)S(1)} %copy-done.8, bf16[1,192,1024]{2,1,0:T(8,128)(2,1)S(1)} %get-tuple-element.99.hidden_ref, bf16[8192,1536]{1,0:T(8,128)(2,1)} %weight_ref.15, bf16[16,4,1536]{2,1,0:T(4,128)(2,1)S(1)} %convert_element_type.365.scale_ref, ...), custom_call_target="tpu_custom_call", output_to_operand_aliasing={{}: (4, {})} | custom-call | flops 18874368 | bytes 98304 | tf_op jit(solution)/shard_map/down/pallas_call | solution.py:110
  144.3 3.2 %down.9.total_ref = f32[192,1536]{1,0:T(8,128)S(1)} custom-call(s32[2,1]{1,0:T(2,128)S(1)} %call_exported.0.index_ref, bf16[1,192,1024]{2,1,0:T(8,128)(2,1)S(1)} %get-tuple-element.97.hidden_ref, bf16[8192,1536]{1,0:T(8,128)(2,1)} %weight_ref.15, bf16[16,4,1536]{2,1,0:T(4,128)(2,1)S(1)} %convert_element_type.365.scale_ref, ...), custom_call_target="tpu_custom_call", output_to_operand_aliasing={{}: (4, {})} | custom-call | flops 18874368 | bytes 98304 | tf_op jit(solution)/shard_map/down/pallas_call | solution.py:110
  149.3 3.2 %down.10.total_ref = f32[192,1536]{1,0:T(8,128)S(1)} custom-call(s32[2,1]{1,0:T(2,128)S(1)} %copy-done.7, bf16[1,192,1024]{2,1,0:T(8,128)(2,1)S(1)} %select_bitcast_fusion.5.hidden_ref, bf16[8192,1536]{1,0:T(8,128)(2,1)} %weight_ref.15, bf16[16,4,1536]{2,1,0:T(4,128)(2,1)S(1)} %convert_element_type.365.scale_ref, ...), custom_call_target="tpu_custom_call", output_to_operand_aliasing={{}: (4, {})} | custom-call | flops 18874368 | bytes 98304 | tf_op jit(solution)/shard_map/down/pallas_call | solution.py:110
  152.5 6.4 %collective-permute-done.18 = bf16[192,1024]{1,0:T(8,128)(2,1)S(1)} collective-permute-done((bf16[192,1024]{1,0:T(8,128)(2,1)S(1)}, bf16[192,1024]{1,0:T(8,128)(2,1)S(1)}, u32[]{:S(2)}, u32[]{:S(2)}) %collective-permute-start.18) | collective-permute-done | bytes 393248 | tf_op jit(solution)/shard_map/ppermute | solution.py:229
  160.5 3.2 %down.11.total_ref = f32[192,1536]{1,0:T(8,128)S(1)} custom-call(s32[2,1]{1,0:T(2,128)S(1)} %copy-done.6, bf16[1,192,1024]{2,1,0:T(8,128)(2,1)S(1)} %select_bitcast_fusion.4.hidden_ref, bf16[8192,1536]{1,0:T(8,128)(2,1)} %weight_ref.15, bf16[16,4,1536]{2,1,0:T(4,128)(2,1)S(1)} %convert_element_type.365.scale_ref, ...), custom_call_target="tpu_custom_call", output_to_operand_aliasing={{}: (4, {})} | custom-call | flops 18874368 | bytes 98304 | tf_op jit(solution)/shard_map/down/pallas_call | solution.py:110
  165.5 3.2 %down.12.total_ref = f32[192,1536]{1,0:T(8,128)S(1)} custom-call(s32[2,1]{1,0:T(2,128)S(1)} %copy-done.5, bf16[1,192,1024]{2,1,0:T(8,128)(2,1)S(1)} %select_bitcast_fusion.3.hidden_ref, bf16[8192,1536]{1,0:T(8,128)(2,1)} %weight_ref.15, bf16[16,4,1536]{2,1,0:T(4,128)(2,1)S(1)} %convert_element_type.365.scale_ref, ...), custom_call_target="tpu_custom_call", output_to_operand_aliasing={{}: (4, {})} | custom-call | flops 18874368 | bytes 98304 | tf_op jit(solution)/shard_map/down/pallas_call | solution.py:110
  170.8 3.2 %down.13.total_ref = f32[192,1536]{1,0:T(8,128)S(1)} custom-call(s32[2,1]{1,0:T(2,128)S(1)} %copy-done.4, bf16[1,192,1024]{2,1,0:T(8,128)(2,1)S(1)} %select_bitcast_fusion.2.hidden_ref, bf16[8192,1536]{1,0:T(8,128)(2,1)} %weight_ref.15, bf16[16,4,1536]{2,1,0:T(4,128)(2,1)S(1)} %convert_element_type.365.scale_ref, ...), custom_call_target="tpu_custom_call", output_to_operand_aliasing={{}: (4, {})} | custom-call | flops 18874368 | bytes 98304 | tf_op jit(solution)/shard_map/down/pallas_call | solution.py:110
  174.7 3.2 %down.14.total_ref = f32[192,1536]{1,0:T(8,128)S(1)} custom-call(s32[2,1]{1,0:T(2,128)S(1)} %copy-done.3, bf16[1,192,1024]{2,1,0:T(8,128)(2,1)S(1)} %select_bitcast_fusion.1.hidden_ref, bf16[8192,1536]{1,0:T(8,128)(2,1)} %weight_ref.15, bf16[16,4,1536]{2,1,0:T(4,128)(2,1)S(1)} %convert_element_type.365.scale_ref, ...), custom_call_target="tpu_custom_call", output_to_operand_aliasing={{}: (4, {})} | custom-call | flops 18874368 | bytes 98304 | tf_op jit(solution)/shard_map/down/pallas_call | solution.py:110
  179.2 3.2 %down.15 = f32[192,1536]{1,0:T(8,128)S(1)} custom-call(s32[2,1]{1,0:T(2,128)S(1)} %copy-done.2, bf16[1,192,1024]{2,1,0:T(8,128)(2,1)S(1)} %select_bitcast_fusion.hidden_ref, bf16[8192,1536]{1,0:T(8,128)(2,1)} %weight_ref.15, bf16[16,4,1536]{2,1,0:T(4,128)(2,1)S(1)} %convert_element_type.365.scale_ref, ...), custom_call_target="tpu_custom_call", output_to_operand_aliasing={{}: (4, {})} | custom-call | flops 18874368 | bytes 98304 | tf_op jit(solution)/shard_map/down/pallas_call | solution.py:110
  182.5 12.8 %all_to_all.23 = bf16[8,24,1536]{2,1,0:T(8,128)(2,1)S(1)} all-to-all(bf16[8,24,1536]{2,1,0:T(8,128)(2,1)S(1)} %bitcast.204), channel_id=1, replica_groups=mesh['fsdp'=4,'expert'=8] {'expert'}, dimensions={0} | all-to-all | bytes 1179648 | tf_op jit(solution)/shard_map/all_to_all | solution.py:269
  (141 shorter events, 75.4 us)
Async XLA Ops:
  4.9 15.6 %all-to-all-start = ((bf16[8,24,1536]{2,1,0:T(8,128)(2,1)}), bf16[8,24,1536]{2,1,0:T(8,128)(2,1)S(1)}, u32[]{:S(2)}, u32[]{:S(2)}) async-start(bf16[8,24,1536]{2,1,0:T(8,128)(2,1)} %bitcast.20), calls=%async_computation | async-start | bytes 1179648 | tf_op jit(solution)/shard_map/all_to_all | solution.py:266
  24.8 12.9 %collective-permute-start = (bf16[2,192,1024]{2,1,0:T(8,128)(2,1)S(1)}, bf16[2,192,1024]{2,1,0:T(8,128)(2,1)S(1)}, u32[]{:S(2)}, u32[]{:S(2)}) collective-permute-start(bf16[2,192,1024]{2,1,0:T(8,128)(2,1)S(1)} %gate_up.14), channel_id=1, source_target_pairs={{0,8},{25,17},{2,10},{27,19},{4,12},{29,21},{6,14},{31,23}} | collective-permute-start | bytes 2359304 | tf_op jit(solution)/shard_map/ppermute | solution.py:214
  31.1 14.2 %collective-permute-start.1 = (bf16[2,192,1024]{2,1,0:T(8,128)(2,1)S(1)}, bf16[2,192,1024]{2,1,0:T(8,128)(2,1)}, u32[]{:S(2)}, u32[]{:S(2)}) collective-permute-start(bf16[2,192,1024]{2,1,0:T(8,128)(2,1)S(1)} %gate_up.15), channel_id=1, source_target_pairs={{0,8},{25,17},{2,10},{27,19},{4,12},{29,21},{6,14},{31,23}} | collective-permute-start | bytes 2359304 | tf_op jit(solution)/shard_map/ppermute | solution.py:214
  38.0 18.7 %collective-permute-start.2 = (bf16[2,192,1024]{2,1,0:T(8,128)(2,1)S(1)}, bf16[2,192,1024]{2,1,0:T(8,128)(2,1)S(1)}, u32[]{:S(2)}, u32[]{:S(2)}) collective-permute-start(bf16[2,192,1024]{2,1,0:T(8,128)(2,1)S(1)} %add_convert_fusion.11), channel_id=1, source_target_pairs={{0,8},{8,16},{25,17},{17,9},{2,10},{10,18},{27,19},{19,11},{4,12},... | collective-permute-start | bytes 2359304 | tf_op jit(solution)/shard_map/ppermute | solution.py:214
  47.6 15.2 %collective-permute-start.3 = (bf16[2,192,1024]{2,1,0:T(8,128)(2,1)}, bf16[2,192,1024]{2,1,0:T(8,128)(2,1)}, u32[]{:S(2)}, u32[]{:S(2)}) collective-permute-start(bf16[2,192,1024]{2,1,0:T(8,128)(2,1)} %add_convert_fusion.10), channel_id=1, source_target_pairs={{0,8},{8,16},{25,17},{17,9},{2,10},{10,18},{27,19},{19,11},{4,12},... | collective-permute-start | bytes 2359304 | tf_op jit(solution)/shard_map/ppermute | solution.py:214
  57.0 16.6 %collective-permute-start.4 = (bf16[2,192,1024]{2,1,0:T(8,128)(2,1)S(1)}, bf16[2,192,1024]{2,1,0:T(8,128)(2,1)S(1)}, u32[]{:S(2)}, u32[]{:S(2)}) collective-permute-start(bf16[2,192,1024]{2,1,0:T(8,128)(2,1)S(1)} %add_convert_fusion.9), channel_id=1, source_target_pairs={{0,8},{8,16},{16,24},{25,17},{17,9},{9,1},{2,10},{10,18},{18,26},{... | collective-permute-start | bytes 2359304 | tf_op jit(solution)/shard_map/ppermute | solution.py:214
  65.1 16.5 %collective-permute-start.5 = (bf16[2,192,1024]{2,1,0:T(8,128)(2,1)}, bf16[2,192,1024]{2,1,0:T(8,128)(2,1)}, u32[]{:S(2)}, u32[]{:S(2)}) collective-permute-start(bf16[2,192,1024]{2,1,0:T(8,128)(2,1)} %add_convert_fusion.8), channel_id=1, source_target_pairs={{0,8},{8,16},{16,24},{25,17},{17,9},{9,1},{2,10},{10,18},{18,26},{... | collective-permute-start | bytes 2359304 | tf_op jit(solution)/shard_map/ppermute | solution.py:214
  74.0 14.2 %collective-permute-start.6 = (bf16[2,192,1024]{2,1,0:T(8,128)(2,1)S(1)}, bf16[2,192,1024]{2,1,0:T(8,128)(2,1)}, u32[]{:S(2)}, u32[]{:S(2)}) collective-permute-start(bf16[2,192,1024]{2,1,0:T(8,128)(2,1)S(1)} %add_convert_fusion.7), channel_id=1, source_target_pairs={{0,8},{8,16},{16,24},{25,17},{17,9},{9,1},{2,10},{10,18},{18,26},{... | collective-permute-start | bytes 2359304 | tf_op jit(solution)/shard_map/ppermute | solution.py:214
  83.0 14.5 %collective-permute-start.10 = (bf16[2,192,1024]{2,1,0:T(8,128)(2,1)S(1)}, bf16[2,192,1024]{2,1,0:T(8,128)(2,1)}, u32[]{:S(2)}, u32[]{:S(2)}) collective-permute-start(bf16[2,192,1024]{2,1,0:T(8,128)(2,1)S(1)} %add_convert_fusion.6), channel_id=1, source_target_pairs={{0,8},{8,16},{16,24},{25,17},{17,9},{9,1},{2,10},{10,18},{18,26},{... | collective-permute-start | bytes 2359304 | tf_op jit(solution)/shard_map/ppermute | solution.py:214
  90.6 11.8 %collective-permute-start.7 = (bf16[2,192,1024]{2,1,0:T(8,128)(2,1)}, bf16[2,192,1024]{2,1,0:T(8,128)(2,1)}, u32[]{:S(2)}, u32[]{:S(2)}) collective-permute-start(bf16[2,192,1024]{2,1,0:T(8,128)(2,1)} %add_convert_fusion.5), channel_id=1, source_target_pairs={{8,16},{16,24},{17,9},{9,1},{10,18},{18,26},{19,11},{11,3},{12,20}... | collective-permute-start | bytes 2359304 | tf_op jit(solution)/shard_map/ppermute | solution.py:214
  92.9 11.6 %collective-permute-start.8 = (bf16[192,1024]{1,0:T(8,128)(2,1)}, bf16[192,1024]{1,0:T(8,128)(2,1)S(1)}, u32[]{:S(2)}, u32[]{:S(2)}) collective-permute-start(bf16[192,1024]{1,0:T(8,128)(2,1)} %fusion.39), channel_id=1, source_target_pairs={{24,16},{1,9},{26,18},{3,11},{28,20},{5,13},{30,22},{7,15}} | collective-permute-start | bytes 1179656 | tf_op jit(solution)/shard_map/ppermute | solution.py:229
  93.6 16.7 %collective-permute-start.11 = (bf16[192,1024]{1,0:T(8,128)(2,1)S(1)}, bf16[192,1024]{1,0:T(8,128)(2,1)S(1)}, u32[]{:S(2)}, u32[]{:S(2)}) collective-permute-start(bf16[192,1024]{1,0:T(8,128)(2,1)S(1)} %fusion.38), channel_id=1, source_target_pairs={{24,16},{1,9},{26,18},{3,11},{28,20},{5,13},{30,22},{7,15}} | collective-permute-start | bytes 1179656 | tf_op jit(solution)/shard_map/ppermute | solution.py:229
  99.0 10.3 %collective-permute-start.12 = (bf16[2,192,1024]{2,1,0:T(8,128)(2,1)S(1)}, bf16[2,192,1024]{2,1,0:T(8,128)(2,1)S(1)}, u32[]{:S(2)}, u32[]{:S(2)}) collective-permute-start(bf16[2,192,1024]{2,1,0:T(8,128)(2,1)S(1)} %add_convert_fusion.3), channel_id=1, source_target_pairs={{8,16},{16,24},{17,9},{9,1},{10,18},{18,26},{19,11},{11,3},{12,20}... | collective-permute-start | bytes 2359304 | tf_op jit(solution)/shard_map/ppermute | solution.py:214
  103.8 10.2 %collective-permute-start.13 = (bf16[2,192,1024]{2,1,0:T(8,128)(2,1)S(1)}, bf16[2,192,1024]{2,1,0:T(8,128)(2,1)S(1)}, u32[]{:S(2)}, u32[]{:S(2)}) collective-permute-start(bf16[2,192,1024]{2,1,0:T(8,128)(2,1)S(1)} %add_convert_fusion.4), channel_id=1, source_target_pairs={{16,24},{9,1},{18,26},{11,3},{20,28},{13,5},{22,30},{15,7}} | collective-permute-start | bytes 2359304 | tf_op jit(solution)/shard_map/ppermute | solution.py:214
  106.0 8.3 %collective-permute-start.9 = (bf16[192,1024]{1,0:T(8,128)(2,1)S(1)}, bf16[192,1024]{1,0:T(8,128)(2,1)S(1)}, u32[]{:S(2)}, u32[]{:S(2)}) collective-permute-start(bf16[192,1024]{1,0:T(8,128)(2,1)S(1)} %fusion.40), channel_id=1, source_target_pairs={{16,8},{24,16},{9,17},{1,9},{18,10},{26,18},{11,19},{3,11},{20,12}... | collective-permute-start | bytes 1179656 | tf_op jit(solution)/shard_map/ppermute | solution.py:229
  109.6 9.0 %collective-permute-start.14 = (bf16[2,192,1024]{2,1,0:T(8,128)(2,1)S(1)}, bf16[2,192,1024]{2,1,0:T(8,128)(2,1)S(1)}, u32[]{:S(2)}, u32[]{:S(2)}) collective-permute-start(bf16[2,192,1024]{2,1,0:T(8,128)(2,1)S(1)} %add_convert_fusion.2), channel_id=1, source_target_pairs={{16,24},{9,1},{18,26},{11,3},{20,28},{13,5},{22,30},{15,7}} | collective-permute-start | bytes 2359304 | tf_op jit(solution)/shard_map/ppermute | solution.py:214
  114.6 20.1 %collective-permute-start.17 = (bf16[192,1024]{1,0:T(8,128)(2,1)S(1)}, bf16[192,1024]{1,0:T(8,128)(2,1)S(1)}, u32[]{:S(2)}, u32[]{:S(2)}) collective-permute-start(bf16[192,1024]{1,0:T(8,128)(2,1)S(1)} %broadcast_select_fusion.3), channel_id=1, source_target_pairs={{8,0},{16,8},{24,16},{17,25},{9,17},{1,9},{10,2},{18,10},{26,18},{... | collective-permute-start | bytes 1179656 | tf_op jit(solution)/shard_map/ppermute | solution.py:229
  119.2 23.1 %collective-permute-start.16 = (bf16[192,1024]{1,0:T(8,128)(2,1)S(1)}, bf16[192,1024]{1,0:T(8,128)(2,1)S(1)}, u32[]{:S(2)}, u32[]{:S(2)}) collective-permute-start(bf16[192,1024]{1,0:T(8,128)(2,1)S(1)} %broadcast_select_fusion.2), channel_id=1, source_target_pairs={{8,0},{16,8},{24,16},{17,25},{9,17},{1,9},{10,2},{18,10},{26,18},{... | collective-permute-start | bytes 1179656 | tf_op jit(solution)/shard_map/ppermute | solution.py:229
  135.5 12.4 %collective-permute-start.19 = (bf16[192,1024]{1,0:T(8,128)(2,1)S(1)}, bf16[192,1024]{1,0:T(8,128)(2,1)S(1)}, u32[]{:S(2)}, u32[]{:S(2)}) collective-permute-start(bf16[192,1024]{1,0:T(8,128)(2,1)S(1)} %get-tuple-element.100), channel_id=1, source_target_pairs={{8,0},{16,8},{24,16},{17,25},{9,17},{1,9},{10,2},{18,10},{26,18},{... | collective-permute-start | bytes 1179656 | tf_op jit(solution)/shard_map/ppermute | solution.py:229
  143.0 15.9 %collective-permute-start.18 = (bf16[192,1024]{1,0:T(8,128)(2,1)S(1)}, bf16[192,1024]{1,0:T(8,128)(2,1)S(1)}, u32[]{:S(2)}, u32[]{:S(2)}) collective-permute-start(bf16[192,1024]{1,0:T(8,128)(2,1)S(1)} %get-tuple-element.98), channel_id=1, source_target_pairs={{8,0},{16,8},{24,16},{17,25},{9,17},{1,9},{10,2},{18,10},{26,18},{... | collective-permute-start | bytes 1179656 | tf_op jit(solution)/shard_map/ppermute | solution.py:229
  147.9 16.2 %collective-permute-start.21 = (bf16[192,1024]{1,0:T(8,128)(2,1)S(1)}, bf16[192,1024]{1,0:T(8,128)(2,1)S(1)}, u32[]{:S(2)}, u32[]{:S(2)}) collective-permute-start(bf16[192,1024]{1,0:T(8,128)(2,1)S(1)} %collective-permute-done.19), channel_id=1, source_target_pairs={{8,0},{16,8},{17,25},{9,17},{10,2},{18,10},{19,27},{11,19},{12,4},... | collective-permute-start | bytes 1179656 | tf_op jit(solution)/shard_map/ppermute | solution.py:229
  158.9 10.5 %collective-permute-start.20 = (bf16[192,1024]{1,0:T(8,128)(2,1)S(1)}, bf16[192,1024]{1,0:T(8,128)(2,1)S(1)}, u32[]{:S(2)}, u32[]{:S(2)}) collective-permute-start(bf16[192,1024]{1,0:T(8,128)(2,1)S(1)} %collective-permute-done.18), channel_id=1, source_target_pairs={{8,0},{16,8},{17,25},{9,17},{10,2},{18,10},{19,27},{11,19},{12,4},... | collective-permute-start | bytes 1179656 | tf_op jit(solution)/shard_map/ppermute | solution.py:229
  164.1 10.2 %collective-permute-start.23 = (bf16[192,1024]{1,0:T(8,128)(2,1)S(1)}, bf16[192,1024]{1,0:T(8,128)(2,1)S(1)}, u32[]{:S(2)}, u32[]{:S(2)}) collective-permute-start(bf16[192,1024]{1,0:T(8,128)(2,1)S(1)} %collective-permute-done.21), channel_id=1, source_target_pairs={{8,0},{17,25},{10,2},{19,27},{12,4},{21,29},{14,6},{23,31}} | collective-permute-start | bytes 1179656 | tf_op jit(solution)/shard_map/ppermute | solution.py:229
  169.4 9.7 %collective-permute-start.22 = (bf16[192,1024]{1,0:T(8,128)(2,1)S(1)}, bf16[192,1024]{1,0:T(8,128)(2,1)S(1)}, u32[]{:S(2)}, u32[]{:S(2)}) collective-permute-start(bf16[192,1024]{1,0:T(8,128)(2,1)S(1)} %collective-permute-done.20), channel_id=1, source_target_pairs={{8,0},{17,25},{10,2},{19,27},{12,4},{21,29},{14,6},{23,31}} | collective-permute-start | bytes 1179656 | tf_op jit(solution)/shard_map/ppermute | solution.py:229
  (14 other events, 95.9 us)

commit v5 on v4

--- a/solution.py
+++ b/solution.py
@@ -256,7 +256,15 @@
     placing = (target[:, None] == jnp.arange(slot_total, dtype=jnp.int32)[None, :]).astype(
         jnp.float32
     )
-    token_map = jnp.sum(placing.reshape(local_tokens, 2, slot_total), axis=1).astype(jnp.bfloat16)
+    numbers = jnp.arange(EXPERTS, dtype=jnp.int32)[None, :]
+    chosen = [(expert_ids[:, k : k + 1] == numbers).astype(jnp.int32) for k in range(2)]
+    prior = jnp.cumsum(chosen[0] + chosen[1], axis=0) - chosen[0] - chosen[1]
+    first, second = [
+        expert_ids[:, k : k + 1] * CAP + jnp.sum(prior * chosen[k], axis=1, keepdims=True)
+        == jnp.arange(slot_total, dtype=jnp.int32)[None, :]
+        for k in range(2)
+    ]
+    token_map = (first | second).astype(jnp.bfloat16)
     packed = jnp.einsum("ts,td->sd", token_map, tokens, preferred_element_type=jnp.float32).astype(
         jnp.bfloat16
     )

time: 198 us -> 200 us (1.010)
  blocking collectives: 12.8 us -> 0 us
  waiting for transfers between devices: 35.6 us -> 44.6 us
  starting transfers between devices: 43.5 us -> 47.3 us
  other arithmetic: 22.4 us -> 24.9 us
    all_to_all x1 -> x0, blocking collectives: 12.8 us -> none  [shards(): lax.all_to_all(partial_rows, 'expert', split_axis=0, concat_axis=0, tiled...]
    all_to_all x0 -> x1, waiting for transfers between devices: none -> 9.59 us  [shards(): lax.all_to_all(partial_rows, 'expert', split_axis=0, concat_axis=0, tiled...]
    all_to_all x0 -> x1, starting transfers between devices: none -> 3.54 us  [shards(): lax.all_to_all(partial_rows, 'expert', split_axis=0, concat_axis=0, tiled...]
  transfers between devices with their start and end apart: 25 -> 26, of which waited for: 10 -> 10; matrix products, arithmetic and copies ran while one was open for 11% -> 12% of each run, Pallas kernels for 35% -> 34%
where the time goes in v5:
time: 200 us; the launch traced here: 199 us
  Pallas kernels  76.1 us (38%)
  starting transfers between devices  47.3 us (24%)
  waiting for transfers between devices  44.6 us (22%)
  other arithmetic  24.9 us (12%)
  local copies, waits for them, and re-layouts  2.9 us (1%)
  matrix products  2.33 us (1%)
    pallas_call x14, Pallas kernels, own_terms(): pl.pallas_call(own_kernel, grid_spec=pltpu.PrefetchScalarGridSpec(num_sca...  50.2 us
    pallas_call x8, Pallas kernels, down_add(): pl.pallas_call(functools.partial(down_kernel, steps=steps), grid_spec=plt...  26 us
    ppermute x12, waiting for transfers between devices, expert_rows(): lax.ppermute(hidden, axes, chain_pairs(stages, experts, moving)[1])  25.4 us
    ppermute x12, starting transfers between devices, expert_rows(): lax.ppermute(sums, axes, chain_pairs(stages, experts, moving)[0])  25.1 us
    ppermute x12, starting transfers between devices, expert_rows(): lax.ppermute(hidden, axes, chain_pairs(stages, experts, moving)[1])  13.5 us
    convert_element_type x12, other arithmetic, expert_rows(): (sums.astype(jnp.float32) + arrived.astype(jnp.float32)).astype(jnp.bfloa...  13.2 us
    all_to_all x1, waiting for transfers between devices, shards(): lax.all_to_all(partial_rows, 'expert', split_axis=0, concat_axis=0, tiled...  9.59 us
    all_to_all x1, waiting for transfers between devices, shards(): lax.all_to_all(outgoing, 'expert', split_axis=0, concat_axis=0, tiled=True)  9.56 us
  transfers between devices with their start and end apart: 26, of which 10 were waited for; matrix products, arithmetic and copies ran while one was open for 12% of the time, Pallas kernels for 34%

profile of v5, /device:TPU:0, one launch (start us, length us, event | category | flops | bytes accessed | tf_op | source)
XLA Modules:
  0.0 199.1 jit_solution(2024577751349222009)
XLA Ops:
  3.1 5.2 %all-to-all-start = ((bf16[8,24,1536]{2,1,0:T(8,128)(2,1)}), bf16[8,24,1536]{2,1,0:T(8,128)(2,1)S(1)}, u32[]{:S(2)}, u32[]{:S(2)}) async-start(bf16[8,24,1536]{2,1,0:T(8,128)(2,1)} %bitcast.26), calls=%async_computation | async-start | bytes 1179648 | tf_op jit(solution)/shard_map/all_to_all | solution.py:274
  9.2 9.6 %all-to-all-done = bf16[8,24,1536]{2,1,0:T(8,128)(2,1)S(1)} async-done(((bf16[8,24,1536]{2,1,0:T(8,128)(2,1)}), bf16[8,24,1536]{2,1,0:T(8,128)(2,1)S(1)}, u32[]{:S(2)}, u32[]{:S(2)}) %all-to-all-start) | async-done | bytes 589856 | tf_op jit(solution)/shard_map/all_to_all | solution.py:274
  18.8 4.3 %gate_up.14 = bf16[2,192,1024]{2,1,0:T(8,128)(2,1)S(1)} custom-call(s32[2]{0:T(128)S(1)} %pad_add_fusion.9.index_ref, bf16[192,1536]{1,0:T(8,128)(2,1)S(1)} %bitcast.177, bf16[1536,8192]{1,0:T(8,128)(2,1)} %gate_ref.27, bf16[1536,8192]{1,0:T(8,128)(2,1)} %up_ref.27, bf16[12,8192]{1,0:T(8,128)(2,1)S(1)} %bitcast.191, bf16[12,8192]{1,0:T(8,128)(2,1)S(1)} %bitcast.205), custom_call_target="tpu_custom_call" | custom-call | flops 37748736 | bytes 196608 | tf_op jit(solution)/shard_map/gate_up/pallas_call | solution.py:56
  25.0 4.3 %gate_up.15 = bf16[2,192,1024]{2,1,0:T(8,128)(2,1)S(1)} custom-call(s32[2]{0:T(128)S(1)} %pad_add_fusion.8.index_ref, bf16[192,1536]{1,0:T(8,128)(2,1)S(1)} %bitcast.178, bf16[1536,8192]{1,0:T(8,128)(2,1)} %gate_ref.27, bf16[1536,8192]{1,0:T(8,128)(2,1)} %up_ref.27, bf16[12,8192]{1,0:T(8,128)(2,1)S(1)} %bitcast.192, bf16[12,8192]{1,0:T(8,128)(2,1)S(1)} %bitcast.206), custom_call_target="tpu_custom_call" | custom-call | flops 37748736 | bytes 196608 | tf_op jit(solution)/shard_map/gate_up/pallas_call | solution.py:56
  31.6 4.3 %gate_up.16 = bf16[2,192,1024]{2,1,0:T(8,128)(2,1)S(1)} custom-call(s32[2]{0:T(128)S(1)} %pad_add_fusion.7.index_ref, bf16[192,1536]{1,0:T(8,128)(2,1)S(1)} %bitcast.179, bf16[1536,8192]{1,0:T(8,128)(2,1)} %gate_ref.27, bf16[1536,8192]{1,0:T(8,128)(2,1)} %up_ref.27, bf16[12,8192]{1,0:T(8,128)(2,1)S(1)} %bitcast.193, bf16[12,8192]{1,0:T(8,128)(2,1)S(1)} %bitcast.207), custom_call_target="tpu_custom_call" | custom-call | flops 37748736 | bytes 196608 | tf_op jit(solution)/shard_map/gate_up/pallas_call | solution.py:56
  39.2 4.3 %gate_up.17 = bf16[2,192,1024]{2,1,0:T(8,128)(2,1)S(1)} custom-call(s32[2]{0:T(128)S(1)} %pad_add_fusion.6.index_ref, bf16[192,1536]{1,0:T(8,128)(2,1)S(1)} %bitcast.180, bf16[1536,8192]{1,0:T(8,128)(2,1)} %gate_ref.27, bf16[1536,8192]{1,0:T(8,128)(2,1)} %up_ref.27, bf16[12,8192]{1,0:T(8,128)(2,1)S(1)} %bitcast.194, bf16[12,8192]{1,0:T(8,128)(2,1)S(1)} %bitcast.208), custom_call_target="tpu_custom_call" | custom-call | flops 37748736 | bytes 196608 | tf_op jit(solution)/shard_map/gate_up/pallas_call | solution.py:56
  45.9 4.7 %collective-permute-start.3 = (bf16[2,192,1024]{2,1,0:T(8,128)(2,1)}, bf16[2,192,1024]{2,1,0:T(8,128)(2,1)}, u32[]{:S(2)}, u32[]{:S(2)}) collective-permute-start(bf16[2,192,1024]{2,1,0:T(8,128)(2,1)} %add_convert_fusion.10), channel_id=1, source_target_pairs={{0,8},{8,16},{25,17},{17,9},{2,10},{10,18},{27,19},{19,11},{4,12},... | collective-permute-start | bytes 2359304 | tf_op jit(solution)/shard_map/ppermute | solution.py:214
  50.6 4.3 %gate_up.18 = bf16[2,192,1024]{2,1,0:T(8,128)(2,1)S(1)} custom-call(s32[2]{0:T(128)S(1)} %pad_add_fusion.5.index_ref, bf16[192,1536]{1,0:T(8,128)(2,1)S(1)} %bitcast.181, bf16[1536,8192]{1,0:T(8,128)(2,1)} %gate_ref.27, bf16[1536,8192]{1,0:T(8,128)(2,1)} %up_ref.27, bf16[12,8192]{1,0:T(8,128)(2,1)S(1)} %bitcast.195, bf16[12,8192]{1,0:T(8,128)(2,1)S(1)} %bitcast.209), custom_call_target="tpu_custom_call" | custom-call | flops 37748736 | bytes 196608 | tf_op jit(solution)/shard_map/gate_up/pallas_call | solution.py:56
  56.7 4.3 %gate_up.19 = bf16[2,192,1024]{2,1,0:T(8,128)(2,1)S(1)} custom-call(s32[2]{0:T(128)S(1)} %pad_add_fusion.4.index_ref, bf16[192,1536]{1,0:T(8,128)(2,1)S(1)} %bitcast.182, bf16[1536,8192]{1,0:T(8,128)(2,1)} %gate_ref.27, bf16[1536,8192]{1,0:T(8,128)(2,1)} %up_ref.27, bf16[12,8192]{1,0:T(8,128)(2,1)S(1)} %bitcast.196, bf16[12,8192]{1,0:T(8,128)(2,1)S(1)} %bitcast.210), custom_call_target="tpu_custom_call" | custom-call | flops 37748736 | bytes 196608 | tf_op jit(solution)/shard_map/gate_up/pallas_call | solution.py:56
  63.3 4.0 %collective-permute-start.5 = (bf16[2,192,1024]{2,1,0:T(8,128)(2,1)}, bf16[2,192,1024]{2,1,0:T(8,128)(2,1)}, u32[]{:S(2)}, u32[]{:S(2)}) collective-permute-start(bf16[2,192,1024]{2,1,0:T(8,128)(2,1)} %add_convert_fusion.8), channel_id=1, source_target_pairs={{0,8},{8,16},{16,24},{25,17},{17,9},{9,1},{2,10},{10,18},{18,26},{... | collective-permute-start | bytes 2359304 | tf_op jit(solution)/shard_map/ppermute | solution.py:214
  67.5 4.3 %gate_up.20 = bf16[2,192,1024]{2,1,0:T(8,128)(2,1)S(1)} custom-call(s32[2]{0:T(128)S(1)} %pad_add_fusion.3.index_ref, bf16[192,1536]{1,0:T(8,128)(2,1)S(1)} %bitcast.183, bf16[1536,8192]{1,0:T(8,128)(2,1)} %gate_ref.27, bf16[1536,8192]{1,0:T(8,128)(2,1)} %up_ref.27, bf16[12,8192]{1,0:T(8,128)(2,1)S(1)} %bitcast.197, bf16[12,8192]{1,0:T(8,128)(2,1)S(1)} %bitcast.211), custom_call_target="tpu_custom_call" | custom-call | flops 37748736 | bytes 196608 | tf_op jit(solution)/shard_map/gate_up/pallas_call | solution.py:56
  75.5 4.3 %gate_up.21 = bf16[2,192,1024]{2,1,0:T(8,128)(2,1)S(1)} custom-call(s32[2]{0:T(128)S(1)} %pad_add_fusion.2.index_ref, bf16[192,1536]{1,0:T(8,128)(2,1)S(1)} %bitcast.184, bf16[1536,8192]{1,0:T(8,128)(2,1)} %gate_ref.27, bf16[1536,8192]{1,0:T(8,128)(2,1)} %up_ref.27, bf16[12,8192]{1,0:T(8,128)(2,1)S(1)} %bitcast.198, bf16[12,8192]{1,0:T(8,128)(2,1)S(1)} %bitcast.212), custom_call_target="tpu_custom_call" | custom-call | flops 37748736 | bytes 196608 | tf_op jit(solution)/shard_map/gate_up/pallas_call | solution.py:56
  119.1 14.2 %collective-permute-done.17 = bf16[192,1024]{1,0:T(8,128)(2,1)S(1)} collective-permute-done((bf16[192,1024]{1,0:T(8,128)(2,1)S(1)}, bf16[192,1024]{1,0:T(8,128)(2,1)S(1)}, u32[]{:S(2)}, u32[]{:S(2)}) %collective-permute-start.17) | collective-permute-done | bytes 393248 | tf_op jit(solution)/shard_map/ppermute | solution.py:229
  136.2 3.2 %down.8.total_ref = f32[192,1536]{1,0:T(8,128)S(1)} custom-call(s32[2,1]{1,0:T(2,128)S(1)} %copy-done.8, bf16[1,192,1024]{2,1,0:T(8,128)(2,1)S(1)} %get-tuple-element.99.hidden_ref, bf16[8192,1536]{1,0:T(8,128)(2,1)} %weight_ref.15, bf16[16,4,1536]{2,1,0:T(4,128)(2,1)S(1)} %convert_element_type.366.scale_ref, ...), custom_call_target="tpu_custom_call", output_to_operand_aliasing={{}: (4, {})} | custom-call | flops 18874368 | bytes 98304 | tf_op jit(solution)/shard_map/down/pallas_call | solution.py:110
  143.3 3.2 %down.9.total_ref = f32[192,1536]{1,0:T(8,128)S(1)} custom-call(s32[2,1]{1,0:T(2,128)S(1)} %call_exported.0.index_ref, bf16[1,192,1024]{2,1,0:T(8,128)(2,1)S(1)} %get-tuple-element.97.hidden_ref, bf16[8192,1536]{1,0:T(8,128)(2,1)} %weight_ref.15, bf16[16,4,1536]{2,1,0:T(4,128)(2,1)S(1)} %convert_element_type.366.scale_ref, ...), custom_call_target="tpu_custom_call", output_to_operand_aliasing={{}: (4, {})} | custom-call | flops 18874368 | bytes 98304 | tf_op jit(solution)/shard_map/down/pallas_call | solution.py:110
  149.9 3.2 %down.10.total_ref = f32[192,1536]{1,0:T(8,128)S(1)} custom-call(s32[2,1]{1,0:T(2,128)S(1)} %copy-done.7, bf16[1,192,1024]{2,1,0:T(8,128)(2,1)S(1)} %select_bitcast_fusion.5.hidden_ref, bf16[8192,1536]{1,0:T(8,128)(2,1)} %weight_ref.15, bf16[16,4,1536]{2,1,0:T(4,128)(2,1)S(1)} %convert_element_type.366.scale_ref, ...), custom_call_target="tpu_custom_call", output_to_operand_aliasing={{}: (4, {})} | custom-call | flops 18874368 | bytes 98304 | tf_op jit(solution)/shard_map/down/pallas_call | solution.py:110
  153.2 4.2 %collective-permute-done.18 = bf16[192,1024]{1,0:T(8,128)(2,1)S(1)} collective-permute-done((bf16[192,1024]{1,0:T(8,128)(2,1)S(1)}, bf16[192,1024]{1,0:T(8,128)(2,1)S(1)}, u32[]{:S(2)}, u32[]{:S(2)}) %collective-permute-start.18) | collective-permute-done | bytes 393248 | tf_op jit(solution)/shard_map/ppermute | solution.py:229
  159.1 3.2 %down.11.total_ref = f32[192,1536]{1,0:T(8,128)S(1)} custom-call(s32[2,1]{1,0:T(2,128)S(1)} %copy-done.6, bf16[1,192,1024]{2,1,0:T(8,128)(2,1)S(1)} %select_bitcast_fusion.4.hidden_ref, bf16[8192,1536]{1,0:T(8,128)(2,1)} %weight_ref.15, bf16[16,4,1536]{2,1,0:T(4,128)(2,1)S(1)} %convert_element_type.366.scale_ref, ...), custom_call_target="tpu_custom_call", output_to_operand_aliasing={{}: (4, {})} | custom-call | flops 18874368 | bytes 98304 | tf_op jit(solution)/shard_map/down/pallas_call | solution.py:110
  164.5 3.2 %down.12.total_ref = f32[192,1536]{1,0:T(8,128)S(1)} custom-call(s32[2,1]{1,0:T(2,128)S(1)} %copy-done.5, bf16[1,192,1024]{2,1,0:T(8,128)(2,1)S(1)} %select_bitcast_fusion.3.hidden_ref, bf16[8192,1536]{1,0:T(8,128)(2,1)} %weight_ref.15, bf16[16,4,1536]{2,1,0:T(4,128)(2,1)S(1)} %convert_element_type.366.scale_ref, ...), custom_call_target="tpu_custom_call", output_to_operand_aliasing={{}: (4, {})} | custom-call | flops 18874368 | bytes 98304 | tf_op jit(solution)/shard_map/down/pallas_call | solution.py:110
  170.6 3.2 %down.13.total_ref = f32[192,1536]{1,0:T(8,128)S(1)} custom-call(s32[2,1]{1,0:T(2,128)S(1)} %copy-done.4, bf16[1,192,1024]{2,1,0:T(8,128)(2,1)S(1)} %select_bitcast_fusion.2.hidden_ref, bf16[8192,1536]{1,0:T(8,128)(2,1)} %weight_ref.15, bf16[16,4,1536]{2,1,0:T(4,128)(2,1)S(1)} %convert_element_type.366.scale_ref, ...), custom_call_target="tpu_custom_call", output_to_operand_aliasing={{}: (4, {})} | custom-call | flops 18874368 | bytes 98304 | tf_op jit(solution)/shard_map/down/pallas_call | solution.py:110
  174.6 3.2 %down.14.total_ref = f32[192,1536]{1,0:T(8,128)S(1)} custom-call(s32[2,1]{1,0:T(2,128)S(1)} %copy-done.3, bf16[1,192,1024]{2,1,0:T(8,128)(2,1)S(1)} %select_bitcast_fusion.1.hidden_ref, bf16[8192,1536]{1,0:T(8,128)(2,1)} %weight_ref.15, bf16[16,4,1536]{2,1,0:T(4,128)(2,1)S(1)} %convert_element_type.366.scale_ref, ...), custom_call_target="tpu_custom_call", output_to_operand_aliasing={{}: (4, {})} | custom-call | flops 18874368 | bytes 98304 | tf_op jit(solution)/shard_map/down/pallas_call | solution.py:110
  180.0 3.3 %down.15 = f32[192,1536]{1,0:T(8,128)S(1)} custom-call(s32[2,1]{1,0:T(2,128)S(1)} %copy-done.2, bf16[1,192,1024]{2,1,0:T(8,128)(2,1)S(1)} %select_bitcast_fusion.hidden_ref, bf16[8192,1536]{1,0:T(8,128)(2,1)} %weight_ref.15, bf16[16,4,1536]{2,1,0:T(4,128)(2,1)S(1)} %convert_element_type.366.scale_ref, ...), custom_call_target="tpu_custom_call", output_to_operand_aliasing={{}: (4, {})} | custom-call | flops 18874368 | bytes 98304 | tf_op jit(solution)/shard_map/down/pallas_call | solution.py:110
  184.1 3.5 %all-to-all-start.1 = ((bf16[8,24,1536]{2,1,0:T(8,128)(2,1)}), bf16[8,24,1536]{2,1,0:T(8,128)(2,1)S(1)}, u32[]{:S(2)}, u32[]{:S(2)}) async-start(bf16[8,24,1536]{2,1,0:T(8,128)(2,1)} %bitcast.68), calls=%async_computation.1 | async-start | bytes 1179648 | tf_op jit(solution)/shard_map/all_to_all | solution.py:277
  188.5 9.6 %all-to-all-done.1 = bf16[8,24,1536]{2,1,0:T(8,128)(2,1)S(1)} async-done(((bf16[8,24,1536]{2,1,0:T(8,128)(2,1)}), bf16[8,24,1536]{2,1,0:T(8,128)(2,1)S(1)}, u32[]{:S(2)}, u32[]{:S(2)}) %all-to-all-start.1) | async-done | bytes 589856 | tf_op jit(solution)/shard_map/all_to_all | solution.py:277
  (161 shorter events, 82.8 us)
Async XLA Ops:
  3.1 15.6 %all-to-all-start = ((bf16[8,24,1536]{2,1,0:T(8,128)(2,1)}), bf16[8,24,1536]{2,1,0:T(8,128)(2,1)S(1)}, u32[]{:S(2)}, u32[]{:S(2)}) async-start(bf16[8,24,1536]{2,1,0:T(8,128)(2,1)} %bitcast.26), calls=%async_computation | async-start | bytes 1179648 | tf_op jit(solution)/shard_map/all_to_all | solution.py:274
  23.1 12.9 %collective-permute-start = (bf16[2,192,1024]{2,1,0:T(8,128)(2,1)S(1)}, bf16[2,192,1024]{2,1,0:T(8,128)(2,1)S(1)}, u32[]{:S(2)}, u32[]{:S(2)}) collective-permute-start(bf16[2,192,1024]{2,1,0:T(8,128)(2,1)S(1)} %gate_up.14), channel_id=1, source_target_pairs={{0,8},{25,17},{2,10},{27,19},{4,12},{29,21},{6,14},{31,23}} | collective-permute-start | bytes 2359304 | tf_op jit(solution)/shard_map/ppermute | solution.py:214
  29.3 14.2 %collective-permute-start.1 = (bf16[2,192,1024]{2,1,0:T(8,128)(2,1)S(1)}, bf16[2,192,1024]{2,1,0:T(8,128)(2,1)}, u32[]{:S(2)}, u32[]{:S(2)}) collective-permute-start(bf16[2,192,1024]{2,1,0:T(8,128)(2,1)S(1)} %gate_up.15), channel_id=1, source_target_pairs={{0,8},{25,17},{2,10},{27,19},{4,12},{29,21},{6,14},{31,23}} | collective-permute-start | bytes 2359304 | tf_op jit(solution)/shard_map/ppermute | solution.py:214
  36.2 18.7 %collective-permute-start.2 = (bf16[2,192,1024]{2,1,0:T(8,128)(2,1)S(1)}, bf16[2,192,1024]{2,1,0:T(8,128)(2,1)S(1)}, u32[]{:S(2)}, u32[]{:S(2)}) collective-permute-start(bf16[2,192,1024]{2,1,0:T(8,128)(2,1)S(1)} %add_convert_fusion.11), channel_id=1, source_target_pairs={{0,8},{8,16},{25,17},{17,9},{2,10},{10,18},{27,19},{19,11},{4,12},... | collective-permute-start | bytes 2359304 | tf_op jit(solution)/shard_map/ppermute | solution.py:214
  45.9 15.1 %collective-permute-start.3 = (bf16[2,192,1024]{2,1,0:T(8,128)(2,1)}, bf16[2,192,1024]{2,1,0:T(8,128)(2,1)}, u32[]{:S(2)}, u32[]{:S(2)}) collective-permute-start(bf16[2,192,1024]{2,1,0:T(8,128)(2,1)} %add_convert_fusion.10), channel_id=1, source_target_pairs={{0,8},{8,16},{25,17},{17,9},{2,10},{10,18},{27,19},{19,11},{4,12},... | collective-permute-start | bytes 2359304 | tf_op jit(solution)/shard_map/ppermute | solution.py:214
  55.2 16.6 %collective-permute-start.4 = (bf16[2,192,1024]{2,1,0:T(8,128)(2,1)S(1)}, bf16[2,192,1024]{2,1,0:T(8,128)(2,1)S(1)}, u32[]{:S(2)}, u32[]{:S(2)}) collective-permute-start(bf16[2,192,1024]{2,1,0:T(8,128)(2,1)S(1)} %add_convert_fusion.9), channel_id=1, source_target_pairs={{0,8},{8,16},{16,24},{25,17},{17,9},{9,1},{2,10},{10,18},{18,26},{... | collective-permute-start | bytes 2359304 | tf_op jit(solution)/shard_map/ppermute | solution.py:214
  63.3 16.5 %collective-permute-start.5 = (bf16[2,192,1024]{2,1,0:T(8,128)(2,1)}, bf16[2,192,1024]{2,1,0:T(8,128)(2,1)}, u32[]{:S(2)}, u32[]{:S(2)}) collective-permute-start(bf16[2,192,1024]{2,1,0:T(8,128)(2,1)} %add_convert_fusion.8), channel_id=1, source_target_pairs={{0,8},{8,16},{16,24},{25,17},{17,9},{9,1},{2,10},{10,18},{18,26},{... | collective-permute-start | bytes 2359304 | tf_op jit(solution)/shard_map/ppermute | solution.py:214
  72.2 14.9 %collective-permute-start.6 = (bf16[2,192,1024]{2,1,0:T(8,128)(2,1)S(1)}, bf16[2,192,1024]{2,1,0:T(8,128)(2,1)}, u32[]{:S(2)}, u32[]{:S(2)}) collective-permute-start(bf16[2,192,1024]{2,1,0:T(8,128)(2,1)S(1)} %add_convert_fusion.7), channel_id=1, source_target_pairs={{0,8},{8,16},{16,24},{25,17},{17,9},{9,1},{2,10},{10,18},{18,26},{... | collective-permute-start | bytes 2359304 | tf_op jit(solution)/shard_map/ppermute | solution.py:214
  81.2 14.8 %collective-permute-start.10 = (bf16[2,192,1024]{2,1,0:T(8,128)(2,1)S(1)}, bf16[2,192,1024]{2,1,0:T(8,128)(2,1)}, u32[]{:S(2)}, u32[]{:S(2)}) collective-permute-start(bf16[2,192,1024]{2,1,0:T(8,128)(2,1)S(1)} %add_convert_fusion.6), channel_id=1, source_target_pairs={{0,8},{8,16},{16,24},{25,17},{17,9},{9,1},{2,10},{10,18},{18,26},{... | collective-permute-start | bytes 2359304 | tf_op jit(solution)/shard_map/ppermute | solution.py:214
  89.4 11.3 %collective-permute-start.7 = (bf16[2,192,1024]{2,1,0:T(8,128)(2,1)}, bf16[2,192,1024]{2,1,0:T(8,128)(2,1)}, u32[]{:S(2)}, u32[]{:S(2)}) collective-permute-start(bf16[2,192,1024]{2,1,0:T(8,128)(2,1)} %add_convert_fusion.5), channel_id=1, source_target_pairs={{8,16},{16,24},{17,9},{9,1},{10,18},{18,26},{19,11},{11,3},{12,20}... | collective-permute-start | bytes 2359304 | tf_op jit(solution)/shard_map/ppermute | solution.py:214
  91.8 11.2 %collective-permute-start.8 = (bf16[192,1024]{1,0:T(8,128)(2,1)}, bf16[192,1024]{1,0:T(8,128)(2,1)S(1)}, u32[]{:S(2)}, u32[]{:S(2)}) collective-permute-start(bf16[192,1024]{1,0:T(8,128)(2,1)} %fusion.39), channel_id=1, source_target_pairs={{24,16},{1,9},{26,18},{3,11},{28,20},{5,13},{30,22},{7,15}} | collective-permute-start | bytes 1179656 | tf_op jit(solution)/shard_map/ppermute | solution.py:229
  92.7 16.1 %collective-permute-start.11 = (bf16[192,1024]{1,0:T(8,128)(2,1)}, bf16[192,1024]{1,0:T(8,128)(2,1)S(1)}, u32[]{:S(2)}, u32[]{:S(2)}) collective-permute-start(bf16[192,1024]{1,0:T(8,128)(2,1)} %fusion.38), channel_id=1, source_target_pairs={{24,16},{1,9},{26,18},{3,11},{28,20},{5,13},{30,22},{7,15}} | collective-permute-start | bytes 1179656 | tf_op jit(solution)/shard_map/ppermute | solution.py:229
  97.4 10.3 %collective-permute-start.12 = (bf16[2,192,1024]{2,1,0:T(8,128)(2,1)S(1)}, bf16[2,192,1024]{2,1,0:T(8,128)(2,1)S(1)}, u32[]{:S(2)}, u32[]{:S(2)}) collective-permute-start(bf16[2,192,1024]{2,1,0:T(8,128)(2,1)S(1)} %add_convert_fusion.3), channel_id=1, source_target_pairs={{8,16},{16,24},{17,9},{9,1},{10,18},{18,26},{19,11},{11,3},{12,20}... | collective-permute-start | bytes 2359304 | tf_op jit(solution)/shard_map/ppermute | solution.py:214
  102.2 10.2 %collective-permute-start.13 = (bf16[2,192,1024]{2,1,0:T(8,128)(2,1)S(1)}, bf16[2,192,1024]{2,1,0:T(8,128)(2,1)S(1)}, u32[]{:S(2)}, u32[]{:S(2)}) collective-permute-start(bf16[2,192,1024]{2,1,0:T(8,128)(2,1)S(1)} %add_convert_fusion.4), channel_id=1, source_target_pairs={{16,24},{9,1},{18,26},{11,3},{20,28},{13,5},{22,30},{15,7}} | collective-permute-start | bytes 2359304 | tf_op jit(solution)/shard_map/ppermute | solution.py:214
  108.1 9.0 %collective-permute-start.14 = (bf16[2,192,1024]{2,1,0:T(8,128)(2,1)S(1)}, bf16[2,192,1024]{2,1,0:T(8,128)(2,1)S(1)}, u32[]{:S(2)}, u32[]{:S(2)}) collective-permute-start(bf16[2,192,1024]{2,1,0:T(8,128)(2,1)S(1)} %add_convert_fusion.2), channel_id=1, source_target_pairs={{16,24},{9,1},{18,26},{11,3},{20,28},{13,5},{22,30},{15,7}} | collective-permute-start | bytes 2359304 | tf_op jit(solution)/shard_map/ppermute | solution.py:214
  113.1 20.2 %collective-permute-start.17 = (bf16[192,1024]{1,0:T(8,128)(2,1)S(1)}, bf16[192,1024]{1,0:T(8,128)(2,1)S(1)}, u32[]{:S(2)}, u32[]{:S(2)}) collective-permute-start(bf16[192,1024]{1,0:T(8,128)(2,1)S(1)} %broadcast_select_fusion.3), channel_id=1, source_target_pairs={{8,0},{16,8},{24,16},{17,25},{9,17},{1,9},{10,2},{18,10},{26,18},{... | collective-permute-start | bytes 1179656 | tf_op jit(solution)/shard_map/ppermute | solution.py:229
  117.7 23.3 %collective-permute-start.16 = (bf16[192,1024]{1,0:T(8,128)(2,1)S(1)}, bf16[192,1024]{1,0:T(8,128)(2,1)S(1)}, u32[]{:S(2)}, u32[]{:S(2)}) collective-permute-start(bf16[192,1024]{1,0:T(8,128)(2,1)S(1)} %broadcast_select_fusion.2), channel_id=1, source_target_pairs={{8,0},{16,8},{24,16},{17,25},{9,17},{1,9},{10,2},{18,10},{26,18},{... | collective-permute-start | bytes 1179656 | tf_op jit(solution)/shard_map/ppermute | solution.py:229
  134.8 12.7 %collective-permute-start.19 = (bf16[192,1024]{1,0:T(8,128)(2,1)}, bf16[192,1024]{1,0:T(8,128)(2,1)}, u32[]{:S(2)}, u32[]{:S(2)}) collective-permute-start(bf16[192,1024]{1,0:T(8,128)(2,1)} %get-tuple-element.100), channel_id=1, source_target_pairs={{8,0},{16,8},{24,16},{17,25},{9,17},{1,9},{10,2},{18,10},{26,18},{... | collective-permute-start | bytes 1179656 | tf_op jit(solution)/shard_map/ppermute | solution.py:229
  141.7 15.7 %collective-permute-start.18 = (bf16[192,1024]{1,0:T(8,128)(2,1)S(1)}, bf16[192,1024]{1,0:T(8,128)(2,1)S(1)}, u32[]{:S(2)}, u32[]{:S(2)}) collective-permute-start(bf16[192,1024]{1,0:T(8,128)(2,1)S(1)} %get-tuple-element.98), channel_id=1, source_target_pairs={{8,0},{16,8},{24,16},{17,25},{9,17},{1,9},{10,2},{18,10},{26,18},{... | collective-permute-start | bytes 1179656 | tf_op jit(solution)/shard_map/ppermute | solution.py:229
  147.5 15.6 %collective-permute-start.21 = (bf16[192,1024]{1,0:T(8,128)(2,1)}, bf16[192,1024]{1,0:T(8,128)(2,1)S(1)}, u32[]{:S(2)}, u32[]{:S(2)}) collective-permute-start(bf16[192,1024]{1,0:T(8,128)(2,1)} %collective-permute-done.19), channel_id=1, source_target_pairs={{8,0},{16,8},{17,25},{9,17},{10,2},{18,10},{19,27},{11,19},{12,4},... | collective-permute-start | bytes 1179656 | tf_op jit(solution)/shard_map/ppermute | solution.py:229
  157.4 11.8 %collective-permute-start.20 = (bf16[192,1024]{1,0:T(8,128)(2,1)S(1)}, bf16[192,1024]{1,0:T(8,128)(2,1)S(1)}, u32[]{:S(2)}, u32[]{:S(2)}) collective-permute-start(bf16[192,1024]{1,0:T(8,128)(2,1)S(1)} %collective-permute-done.18), channel_id=1, source_target_pairs={{8,0},{16,8},{17,25},{9,17},{10,2},{18,10},{19,27},{11,19},{12,4},... | collective-permute-start | bytes 1179656 | tf_op jit(solution)/shard_map/ppermute | solution.py:229
  163.1 11.0 %collective-permute-start.23 = (bf16[192,1024]{1,0:T(8,128)(2,1)S(1)}, bf16[192,1024]{1,0:T(8,128)(2,1)S(1)}, u32[]{:S(2)}, u32[]{:S(2)}) collective-permute-start(bf16[192,1024]{1,0:T(8,128)(2,1)S(1)} %collective-permute-done.21), channel_id=1, source_target_pairs={{8,0},{17,25},{10,2},{19,27},{12,4},{21,29},{14,6},{23,31}} | collective-permute-start | bytes 1179656 | tf_op jit(solution)/shard_map/ppermute | solution.py:229
  169.2 10.6 %collective-permute-start.22 = (bf16[192,1024]{1,0:T(8,128)(2,1)S(1)}, bf16[192,1024]{1,0:T(8,128)(2,1)S(1)}, u32[]{:S(2)}, u32[]{:S(2)}) collective-permute-start(bf16[192,1024]{1,0:T(8,128)(2,1)S(1)} %collective-permute-done.20), channel_id=1, source_target_pairs={{8,0},{17,25},{10,2},{19,27},{12,4},{21,29},{14,6},{23,31}} | collective-permute-start | bytes 1179656 | tf_op jit(solution)/shard_map/ppermute | solution.py:229
  184.1 13.9 %all-to-all-start.1 = ((bf16[8,24,1536]{2,1,0:T(8,128)(2,1)}), bf16[8,24,1536]{2,1,0:T(8,128)(2,1)S(1)}, u32[]{:S(2)}, u32[]{:S(2)}) async-start(bf16[8,24,1536]{2,1,0:T(8,128)(2,1)} %bitcast.68), calls=%async_computation.1 | async-start | bytes 1179648 | tf_op jit(solution)/shard_map/all_to_all | solution.py:277
  (22 other events, 205.4 us)
